TPU v7x, 32 devices: a whole 2x2x4 slice. The times are simulated.
32 devices in a mesh: wide: 16 (over z, y, x), narrow: 2 (over core).
Axes of the slice: x: 2, y: 2, z: 4, core: 2. Of those that a mesh axis runs over, the one named last changes fastest.
Arguments:
- tokens: bfloat16 [1024, 2, 5120], P('wide', None, 'narrow'), may hold values from -6 to 6
- qkv_weight: bfloat16 [5120, 6144], P('wide', 'narrow'), may hold values from -0.078125 to 0.078125
- rotated_prefix_keys: bfloat16 [16, 2048, 1024], P('wide', None, 'narrow'), may hold values from -120 to 120
- shared_prefix_values: bfloat16 [16, 2048, 1024], P('wide', None, 'narrow'), may hold values from -6 to 6
- prefix_of: int32 [1024, 1], P('wide'), may hold values from 0 to 15; in each aligned block of 64 rows (0 to 63, 64 to 127, ...) at most 8 rows name the same one
- positions: int32 [1024], P('wide'), may hold values from 512 to 2048, as said below
Outputs:
- attended: bfloat16 [1024, 2, 4096], P('wide', None, 'narrow')
Inputs may be any that keep to these rules, and one draw needn't show every extreme that they name: `prefix_of`: the 64 requests of one index of wide name each prefix at most 8 times, a bound that some block reaches. The new tokens of request r sit at positions[r] + s.
All inputs are finite; a program needn't handle non-finite values.
Results may differ from a plain program's by a relative error of at most 0.012.
The roundings to bfloat16 on the way count: a program that leaves them out, or rounds other values in their place, can miss the bound.
Values may be sent and summed in bfloat16 or wider, within the bound.
No kernel may reach another device: no remote copies, remote signals or barrier semaphores. Data moves between devices by JAX's collectives and lax.ppermute only.
A program may use at most 128 MiB of HBM per device.

v0:
```python
import jax
import jax.numpy as jnp
from jax import lax
from jax.sharding import PartitionSpec as P

QUERY_HEADS = 32
KEY_VALUE_HEADS = 8
HEAD_SIZE = 128
DECODE_STEPS = 2


def rotate(value_block, where):
    half = HEAD_SIZE // 2
    freq = 10000.0 ** (-(jnp.arange(half, dtype=jnp.float32) * 2.0 / HEAD_SIZE))
    angle = where[..., None].astype(jnp.float32) * freq
    cosine = jnp.cos(angle)
    sine = jnp.sin(angle)
    first_index = value_block[..., :half]
    second = value_block[..., half:]
    return jnp.concatenate(
        [first_index * cosine - second * sine, second * cosine + first_index * sine], axis=-1
    )


def prefix_part(asked, bounds, key_rows, value_block):
    scale = 1.0 / HEAD_SIZE**0.5
    far = (
        jnp.einsum("nskgd,lkd->nskgl", asked, key_rows, preferred_element_type=jnp.float32) * scale
    )
    allowed = jnp.arange(key_rows.shape[0], dtype=jnp.int32)[None, :] < bounds[:, None]
    far = jnp.where(allowed[:, None, None, None, :], far, -1e30)
    top = jnp.max(far, axis=-1)
    weight = jnp.exp(far - top[..., None])
    total = jnp.sum(weight, axis=-1)
    summed = jnp.einsum(
        "nskgl,lkd->nskgd",
        weight.astype(jnp.bfloat16),
        value_block,
        preferred_element_type=jnp.float32,
    )
    return (summed, top, total)


def own_part(asked, near_keys, near_values):
    scale = 1.0 / HEAD_SIZE**0.5
    near = (
        jnp.einsum("nskgd,ntkd->nskgt", asked, near_keys, preferred_element_type=jnp.float32)
        * scale
    )
    causal = jnp.arange(DECODE_STEPS)[:, None] >= jnp.arange(DECODE_STEPS)[None, :]
    near = jnp.where(causal[None, :, None, None, :], near, -1e30)
    top = jnp.max(near, axis=-1)
    weight = jnp.exp(near - top[..., None])
    total = jnp.sum(weight, axis=-1)
    summed = jnp.einsum(
        "nskgt,ntkd->nskgd",
        weight.astype(jnp.bfloat16),
        near_values,
        preferred_element_type=jnp.float32,
    )
    return (summed, top, total)


def combine(first_index, second):
    top = jnp.maximum(first_index[1], second[1])
    left = jnp.exp(first_index[1] - top)
    right = jnp.exp(second[1] - top)
    summed = first_index[0] * left[..., None] + second[0] * right[..., None]
    return (summed, top, first_index[2] * left + second[2] * right)


def fold_rows(inputs, piece):
    return jnp.dot(inputs, piece, preferred_element_type=jnp.float32)


def on_device(tokens, qkv_weight, rotated_prefix_keys, shared_prefix_values, prefix_of, positions):
    rows_dev = tokens.shape[0]
    owners = lax.axis_size("wide")
    capacity = max(2, (2 * rows_dev + owners - 1) // owners)
    kv_local = rotated_prefix_keys.shape[2] // HEAD_SIZE
    query_group = QUERY_HEADS // KEY_VALUE_HEADS
    whole = lax.all_gather(tokens, "narrow", axis=2, tiled=True)
    inputs = whole.reshape(rows_dev * DECODE_STEPS, whole.shape[2])
    mixed_output = fold_rows(inputs, lax.all_gather(qkv_weight, "wide", axis=0, tiled=True))
    mixed_output = mixed_output.reshape(
        rows_dev, DECODE_STEPS, kv_local, query_group + 2, HEAD_SIZE
    )
    where = positions[:, None] + jnp.arange(DECODE_STEPS, dtype=jnp.int32)[None, :]
    query = rotate(mixed_output[:, :, :, :query_group, :], where[:, :, None, None]).astype(
        jnp.bfloat16
    )
    own_key = rotate(mixed_output[:, :, :, query_group, :], where[:, :, None]).astype(jnp.bfloat16)
    own_value = mixed_output[:, :, :, query_group + 1, :].astype(jnp.bfloat16)
    chosen_prefix = prefix_of[:, 0]
    hits = (chosen_prefix[:, None] == jnp.arange(owners, dtype=jnp.int32)[None, :]).astype(
        jnp.int32
    )
    rank = jnp.sum((jnp.cumsum(hits, axis=0) - hits) * hits, axis=1)
    target = chosen_prefix * capacity + rank
    slots = owners * capacity
    dispatch = target[None, :] == jnp.arange(slots, dtype=jnp.int32)[:, None]
    route = dispatch.astype(jnp.bfloat16)
    limits = jnp.sum(jnp.where(dispatch, positions[None, :], 0), axis=1).reshape(owners, capacity)
    key_rows = rotated_prefix_keys[0].reshape(-1, kv_local, HEAD_SIZE)
    value_block = shared_prefix_values[0].reshape(-1, kv_local, HEAD_SIZE)
    flat = query.reshape(rows_dev, -1)
    packed = jnp.dot(route, flat, preferred_element_type=jnp.float32).astype(jnp.bfloat16)
    asked = lax.all_to_all(
        packed.reshape(owners, capacity, flat.shape[1]),
        "wide",
        split_axis=0,
        concat_axis=0,
        tiled=True,
    )
    bounds = lax.all_to_all(limits, "wide", split_axis=0, concat_axis=0, tiled=True)
    count = asked.shape[1]
    items = owners * count
    summed, top, total = prefix_part(
        asked.reshape(items, DECODE_STEPS, kv_local, query_group, HEAD_SIZE),
        bounds.reshape(items),
        key_rows,
        value_block,
    )
    summed, top, total = (
        lax.all_to_all(
            summed.reshape(owners, count, -1).astype(jnp.bfloat16),
            "wide",
            split_axis=0,
            concat_axis=0,
            tiled=True,
        ).astype(jnp.float32),
        lax.all_to_all(
            top.reshape(owners, count, -1).astype(jnp.bfloat16),
            "wide",
            split_axis=0,
            concat_axis=0,
            tiled=True,
        ).astype(jnp.float32),
        lax.all_to_all(
            total.reshape(owners, count, -1).astype(jnp.bfloat16),
            "wide",
            split_axis=0,
            concat_axis=0,
            tiled=True,
        ).astype(jnp.float32),
    )
    far = (
        jnp.take(summed.reshape(slots, -1), target, axis=0).reshape(
            rows_dev, DECODE_STEPS, kv_local, query_group, HEAD_SIZE
        ),
        jnp.take(top.reshape(slots, -1), target, axis=0).reshape(
            rows_dev, DECODE_STEPS, kv_local, query_group
        ),
        jnp.take(total.reshape(slots, -1), target, axis=0).reshape(
            rows_dev, DECODE_STEPS, kv_local, query_group
        ),
    )
    near = own_part(query, own_key, own_value)
    merged, merged_top, merged_total = combine(far, near)
    result = merged / merged_total[..., None]
    return result.astype(jnp.bfloat16).reshape(
        rows_dev, DECODE_STEPS, kv_local * query_group * HEAD_SIZE
    )


def solution(mesh):
    return jax.shard_map(
        on_device,
        mesh=mesh,
        in_specs=(
            P("wide", None, "narrow"),
            P("wide", "narrow"),
            P("wide", None, "narrow"),
            P("wide", None, "narrow"),
            P("wide", None),
            P("wide"),
        ),
        out_specs=P("wide", None, "narrow"),
        check_vma=False,
    )
```

profile of v0, /device:TPU:0, one launch (start us, length us, event | category | flops | bytes accessed | tf_op | source)
XLA Modules:
  0.0 541.9 jit_solution(6912560631890565164)
XLA Ops:
  6.5 0.7 all-gather.5.cloned.1.call-update
  7.3 2.0 copy.86
  9.3 0.7 fusion.38
  10.2 0.8 select_reduce_fusion.1
  11.0 1.2 compare_and_fusion
  12.2 0.7 select_reduce_fusion
  13.0 0.7 all_to_all.18
  13.7 8.3 %all-to-all-start = ((s32[16,1,8]{2,1,0:T(1,128)}), s32[16,1,8]{2,1,0:T(1,128)S(1)}, u32[]{:S(2)}, u32[]{:S(2)}) async-start(s32[16,1,8]{2,1,0:T(1,128)} %bitcast.3), calls=%async_computation | async-start | bytes 16384 | tf_op jit(solution)/shard_map/all_to_all | solution.py:115
  22.0 0.7 add_convert_fusion.1
  23.0 320.9 %all-gather.5.cloned.1.call-done = bf16[5120,3072]{1,0:T(8,128)(2,1)} async-done(((bf16[320,3072]{1,0:T(8,128)(2,1)}), bf16[5120,3072]{1,0:T(8,128)(2,1)}) %all-gather.5.cloned.1.call-update) | async-done | bytes 31457296 | tf_op jit(solution)/shard_map/all_gather | solution.py:84
  343.9 39.0 %copy.87 = bf16[3072,5120]{1,0:T(8,128)(2,1)} copy(bf16[3072,5120]{0,1:T(8,128)(2,1)} %bitcast.88) | data formatting | bytes 62914560 | tf_op jit(solution)/shard_map/dot_general | solution.py:73
  382.9 15.5 %fusion.22 = f32[64,2,4,6,128]{4,0,3,2,1:T(8,128)S(1)} fusion(bf16[4,6,128,5120,1]{3,2,1,0,4:T(8,128)(2,1)} %bitcast.87, bf16[64,2,5120]{2,0,1:T(8,128)(2,1)} %all-gather.3.cloned.1.call-done), kind=kOutput, calls=%fused_computation.21 | convolution fusion | flops 4026531840 | bytes 34340864 | tf_op jit(solution)/shard_map/dot_general | solution.py:73
  399.1 0.8 copy-done
  400.7 1.5 fusion.6
  402.2 4.3 all-to-all-start.1
  406.6 4.0 reshape_squeeze.6
  410.5 0.6 pad_clamp_fusion
  411.1 0.5 and_bitcast_fusion
  411.6 0.6 pad_clamp_fusion.1
  412.2 0.6 broadcast.155
  412.8 0.6 reduce.3
  413.8 16.5 %all-to-all-done.1 = bf16[16,8,4096]{2,1,0:T(8,128)(2,1)} async-done(((bf16[16,8,4096]{2,1,0:T(8,128)(2,1)}), bf16[16,8,4096]{2,1,0:T(8,128)(2,1)}, u32[]{:S(2)}, u32[]{:S(2)}) %all-to-all-start.1) | async-done | bytes 1048608 | tf_op jit(solution)/shard_map/all_to_all | solution.py:108
  430.2 1.8 reshape.226
  432.0 15.8 %bitcast_reduce_fusion = (f32[128,2,4,4]{0,3,1,2:T(4,128)S(1)}, f32[4,128,2,4,2048]{4,1,3,2,0:T(8,128)}) fusion(pred[128,2048]{1,0:T(8,128)(4,1)S(1)} %iota_compare_fusion, bf16[2048,4,128,1,1]{2,1,0,4,3:T(4,128)(2,1)} %bitcast.89, bf16[128,2,4,4,128]{4,3,2,1,0:T(4,128)(2,1)S(1)} %reshape.226), kind=kOutput, calls=%fused_computation.4 | convolution fusion | flops 2172645376 | bytes 36978688 | tf_op jit(solution)/shard_map/nskgd,lkd->nskgl/dot_general | solution.py:28
  447.8 15.0 %fusion.1 = bf16[128,2,4,4]{0,3,1,2:T(4,128)(2,1)S(1)} fusion(f32[4,128,2,4,2048]{4,1,3,2,0:T(8,128)} %get-tuple-element.22, f32[128,2,4,4]{0,3,1,2:T(4,128)S(1)} %get-tuple-element.21, pred[128,2048]{1,0:T(8,128)(4,1)S(1)} %iota_compare_fusion), kind=kLoop, calls=%fused_computation.7 | loop fusion | flops 33550336 | bytes 33841152 | tf_op jit(solution)/shard_map/reduce_sum | solution.py:34
  463.2 0.7 reshape.290
  463.9 5.8 %all-to-all-start.4 = ((bf16[16,2,128]{2,1,0:T(2,128)(2,1)}), bf16[16,2,128]{2,1,0:T(2,128)(2,1)S(1)}, u32[]{:S(2)}, u32[]{:S(2)}) async-start(bf16[16,2,128]{2,1,0:T(2,128)(2,1)} %reshape.290), calls=%async_computation.4 | async-start | bytes 16384 | tf_op jit(solution)/shard_map/all_to_all | solution.py:139
  469.7 4.0 reshape_squeeze.7
  474.1 0.7 reshape.288
  474.8 2.2 all-to-all-done.4
  477.0 4.7 all-to-all-start.3
  481.7 14.7 %fusion.17 = bf16[128,2,4,4,128]{4,0,3,1,2:T(8,128)(2,1)S(1)} fusion(bf16[2048,4,128,1,1]{2,1,0,4,3:T(4,128)(2,1)} %bitcast.90, f32[4,128,2,4,2048]{4,1,3,2,0:T(8,128)} %get-tuple-element.22, f32[128,2,4,4]{0,3,1,2:T(4,128)S(1)} %get-tuple-element.21, pred[128,2048]{1,0:T(8,128)(4,1)S(1)} %iota_compare_fusion), kind=kOutput, calls=%fused_computation.20 | convolution fusion | flops 2181562368 | bytes 36978688 | tf_op jit(solution)/shard_map/nskgl,lkd->nskgd/dot_general | solution.py:35
  496.4 0.8 copy.92
  497.2 1.6 convert_element_type.74
  498.8 6.9 %all-to-all-start.2 = ((bf16[16,8,4096]{2,1,0:T(8,128)(2,1)}), bf16[16,8,4096]{2,1,0:T(8,128)(2,1)S(1)}, u32[]{:S(2)}, u32[]{:S(2)}) async-start(bf16[16,8,4096]{2,1,0:T(8,128)(2,1)} %convert_element_type.74), calls=%async_computation.2 | async-start | bytes 2097152 | tf_op jit(solution)/shard_map/all_to_all | solution.py:125
  506.0 6.7 %fusion.46 = (f32[64,2,4,4]{3,1,2,0:T(2,128)S(1)}, f32[64,2,4,4,2]{3,4,1,2,0:T(2,128)}) fusion(bf16[64,2,4,4,128]{4,0,3,2,1:T(8,128)(2,1)} %copy-done, bf16[64,2,4,128,1]{3,0,2,1,4:T(8,128)(2,1)S(1)} %maximum_bitcast_fusion, pred[2,2]{1,0:T(4,128)(4,1)S(1)} %iota_compare_fusion.4), kind=kOutput, calls=%fused_computation.79 | convolution fusion | flops 1058816 | bytes 679940 | tf_op jit(solution)/shard_map/nskgd,ntkd->nskgt/dot_general | solution.py:47
  512.9 2.1 fusion.31
  515.3 0.7 gather_fusion.2
  516.1 0.7 gather_fusion.1
  516.9 0.7 broadcast_select_fusion.1
  517.7 0.9 copy.100
  518.6 0.9 copy.103
  519.5 0.9 copy.108
  520.3 8.0 %all-to-all-done.2 = bf16[16,8,4096]{2,1,0:T(8,128)(2,1)S(1)} async-done(((bf16[16,8,4096]{2,1,0:T(8,128)(2,1)}), bf16[16,8,4096]{2,1,0:T(8,128)(2,1)S(1)}, u32[]{:S(2)}, u32[]{:S(2)}) %all-to-all-start.2) | async-done | bytes 1048608 | tf_op jit(solution)/shard_map/all_to_all | solution.py:125
  528.5 1.0 gather_fusion
  529.6 0.7 gather.10
  530.3 3.6 fusion.27
  534.1 0.9 reshape.278
  (42 shorter events, 4.4 us)
Async XLA Ops:
  6.5 337.4 %all-gather.5.cloned.1.call-start = ((), (), s32[]{:S(2)}) async-start(), calls=%async_computation.6 | async-start | bytes 33423360 | tf_op jit(solution)/shard_map/all_gather | solution.py:84
  7.3 375.6 %all-gather.3.cloned.1.call-start = ((), (), s32[]{:S(2)}) async-start(), calls=%async_computation.5 | async-start | bytes 1966080 | tf_op jit(solution)/shard_map/all_gather | solution.py:82
  13.7 388.6 %all-to-all-start = ((s32[16,1,8]{2,1,0:T(1,128)}), s32[16,1,8]{2,1,0:T(1,128)S(1)}, u32[]{:S(2)}, u32[]{:S(2)}) async-start(s32[16,1,8]{2,1,0:T(1,128)} %bitcast.3), calls=%async_computation | async-start | bytes 16384 | tf_op jit(solution)/shard_map/all_to_all | solution.py:115
  382.9 28.3 %copy-start.1 = (s32[64,1]{0,1:T(1,128)S(1)}, s32[64,1]{0,1:T(1,128)}, u32[]{:S(2)}) copy-start(s32[64,1]{0,1:T(1,128)} %param.12) | copy-start | bytes 772
  399.1 0.8 copy-start
  402.2 28.0 %all-to-all-start.1 = ((bf16[16,8,4096]{2,1,0:T(8,128)(2,1)}), bf16[16,8,4096]{2,1,0:T(8,128)(2,1)}, u32[]{:S(2)}, u32[]{:S(2)}) async-start(bf16[16,8,4096]{2,1,0:T(8,128)(2,1)} %fusion.6), calls=%async_computation.1 | async-start | bytes 2097152 | tf_op jit(solution)/shard_map/all_to_all | solution.py:108
  463.9 13.1 %all-to-all-start.4 = ((bf16[16,2,128]{2,1,0:T(2,128)(2,1)}), bf16[16,2,128]{2,1,0:T(2,128)(2,1)S(1)}, u32[]{:S(2)}, u32[]{:S(2)}) async-start(bf16[16,2,128]{2,1,0:T(2,128)(2,1)} %reshape.290), calls=%async_computation.4 | async-start | bytes 16384 | tf_op jit(solution)/shard_map/all_to_all | solution.py:139
  477.0 21.9 %all-to-all-start.3 = ((bf16[16,2,128]{2,1,0:T(2,128)(2,1)}), bf16[16,2,128]{2,1,0:T(2,128)(2,1)S(1)}, u32[]{:S(2)}, u32[]{:S(2)}) async-start(bf16[16,2,128]{2,1,0:T(2,128)(2,1)} %reshape.288), calls=%async_computation.3 | async-start | bytes 16384 | tf_op jit(solution)/shard_map/all_to_all | solution.py:132
  498.8 29.5 %all-to-all-start.2 = ((bf16[16,8,4096]{2,1,0:T(8,128)(2,1)}), bf16[16,8,4096]{2,1,0:T(8,128)(2,1)S(1)}, u32[]{:S(2)}, u32[]{:S(2)}) async-start(bf16[16,8,4096]{2,1,0:T(8,128)(2,1)} %convert_element_type.74), calls=%async_computation.2 | async-start | bytes 2097152 | tf_op jit(solution)/shard_map/all_to_all | solution.py:125
Sparse Core Ops, SparseCore 0:
  10.2 333.7 all-gather.4
  345.5 7.5 all-gather.2
where the time goes:
time: 544 us; the launch traced here: 542 us
  waiting for transfers between devices  348 us (64%)
  local copies, waits for them, and re-layouts  65.7 us (12%)
  matrix products  57.9 us (11%)
  starting transfers between devices  30.1 us (6%)
  other arithmetic  26.3 us (5%)
  between operations  13.7 us (3%)
    all_gather x1, waiting for transfers between devices, on_device(): lax.all_gather(qkv_weight, 'wide', axis=0, tiled=True)  321 us
    dot_general x1, local copies, waits for them, and re-layouts, fold_rows(): return jnp.dot(inputs, piece, preferred_element_type=jnp.float32)  39 us
    all_to_all x1, waiting for transfers between devices, on_device(): lax.all_to_all(packed.reshape(owners, capacity, flat.shape[1]), 'wide', s...  16.5 us
    dot_general x1, matrix products, prefix_part(): jnp.einsum('nskgd,lkd->nskgl', asked, key_rows, preferred_element_type=jn...  15.8 us
    dot_general x1, matrix products, fold_rows(): return jnp.dot(inputs, piece, preferred_element_type=jnp.float32)  15.5 us
    reduce_sum x1, other arithmetic, prefix_part(): total = jnp.sum(weight, axis=-1)  15 us
    dot_general x1, matrix products, prefix_part(): jnp.einsum('nskgl,lkd->nskgd', weight.astype(jnp.bfloat16), value_block,...  14.7 us
  transfers between devices with their start and end apart: 7, of which 4 were waited for; matrix products, arithmetic and copies ran while one was open for 20% of the time, Pallas kernels for 0%

commit v1 on v0

v1 whole, which is shorter than its diff:
```python
import functools

import jax
import jax.numpy as jnp
from jax import lax
from jax.experimental import pallas as pl
from jax.experimental.pallas import tpu as pltpu
from jax.sharding import PartitionSpec as P

QUERY_HEADS = 32
KEY_VALUE_HEADS = 8
HEAD_SIZE = 128
DECODE_STEPS = 2
GROUP = QUERY_HEADS // KEY_VALUE_HEADS
SCALE = 1.0 / HEAD_SIZE**0.5
FLOOR = 512
PIECES = 3
NT = (((1,), (1,)), ((), ()))
NN = (((1,), (0,)), ((), ()))


def dot(left, right, dims=NN):
    return lax.dot_general(left, right, dims, preferred_element_type=jnp.float32)


def whole_specs(count):
    return [pl.BlockSpec(memory_space=pltpu.VMEM)] * count


def prefix_kernel(tile, asked, limit, keys, values, out):
    rows = asked.shape[0]
    length = keys.shape[0]
    heads = keys.shape[1] // HEAD_SIZE
    bound = limit[...]
    lane = lax.broadcasted_iota(jnp.int32, (rows, HEAD_SIZE), 1)
    stat = jnp.zeros((rows, HEAD_SIZE), jnp.float32)
    for head in range(heads):
        key_at = slice(head * HEAD_SIZE, (head + 1) * HEAD_SIZE)
        for member in range(GROUP):
            column = head * GROUP + member
            at = slice(column * HEAD_SIZE, (column + 1) * HEAD_SIZE)
            query = asked[:, at]
            parts = []
            top = None
            for start in range(0, length, tile):
                score = dot(query, keys[start : start + tile, key_at], NT)
                if start + tile > FLOOR:
                    where = start + lax.broadcasted_iota(jnp.int32, score.shape, 1)
                    score = jnp.where(where < bound, score, -1e30)
                parts.append(score)
                high = jnp.max(score, axis=1, keepdims=True)
                top = high if top is None else jnp.maximum(top, high)
            total = jnp.zeros((rows, 1), jnp.float32)
            summed = jnp.zeros((rows, HEAD_SIZE), jnp.float32)
            for index, start in enumerate(range(0, length, tile)):
                weight = jnp.exp((parts[index] - top) * SCALE)
                total = total + jnp.sum(weight, axis=1, keepdims=True)
                summed = summed + dot(
                    weight.astype(jnp.bfloat16), values[start : start + tile, key_at]
                )
            out[:, at] = (summed / total).astype(jnp.bfloat16)
            left = top * SCALE + jnp.log(total)
            for piece in range(PIECES):
                part = left.astype(jnp.bfloat16).astype(jnp.float32)
                stat = jnp.where(lane == piece * heads * GROUP + column, part, stat)
                left = left - part
    out[:, heads * GROUP * HEAD_SIZE :] = stat.astype(jnp.bfloat16)


def prefix_part(asked, limit, keys, values, first, heads):
    rows, width = asked.shape
    length = keys.shape[0]
    block = pl.BlockSpec((length, heads * HEAD_SIZE), lambda i: (0, first // heads))
    return pl.pallas_call(
        functools.partial(prefix_kernel, min(length, 512)),
        grid=(1,),
        out_shape=jax.ShapeDtypeStruct((rows, width + HEAD_SIZE), jnp.bfloat16),
        in_specs=[
            pl.BlockSpec((rows, width), lambda i: (0, 0)),
            pl.BlockSpec((rows, 1), lambda i: (0, 0)),
            block,
            block,
        ],
        out_specs=pl.BlockSpec((rows, width + HEAD_SIZE), lambda i: (0, 0)),
        compiler_params=pltpu.CompilerParams(vmem_limit_bytes=40 * 2**20),
        cost_estimate=pl.CostEstimate(
            flops=4 * rows * length * width,
            bytes_accessed=4 * length * heads * HEAD_SIZE,
            transcendentals=rows * length * heads * GROUP,
        ),
        name="prefix_part",
    )(asked, limit, keys, values)


def pack_kernel(count, *refs):
    parts, (cosine, sine, route, asked, query, key, value) = refs[:count], refs[count:]
    heads = key.shape[1] // HEAD_SIZE

    def column(index):
        at = slice(index * HEAD_SIZE, (index + 1) * HEAD_SIZE)
        total = parts[0][:, at].astype(jnp.float32)
        for part in parts[1:]:
            total = total + part[:, at].astype(jnp.float32)
        return total

    def rotated(block):
        turned = pltpu.roll(block, HEAD_SIZE // 2, 1)
        return (block * cosine[...] + turned * sine[...]).astype(jnp.bfloat16)

    for head in range(heads):
        base = head * (GROUP + 2)
        for member in range(GROUP):
            at = head * GROUP + member
            query[:, at * HEAD_SIZE : (at + 1) * HEAD_SIZE] = rotated(column(base + member))
        at = slice(head * HEAD_SIZE, (head + 1) * HEAD_SIZE)
        key[:, at] = rotated(column(base + GROUP))
        value[:, at] = column(base + GROUP + 1).astype(jnp.bfloat16)
    asked[...] = dot(route[...], query[...]).astype(jnp.bfloat16)


def pack(parts, cosine, sine, route, heads):
    rows = cosine.shape[0]
    slots = route.shape[0]
    wide_q, wide_k = heads * GROUP * HEAD_SIZE, heads * HEAD_SIZE
    return pl.pallas_call(
        functools.partial(pack_kernel, len(parts)),
        out_shape=[
            jax.ShapeDtypeStruct((slots, wide_q), jnp.bfloat16),
            jax.ShapeDtypeStruct((rows, wide_q), jnp.bfloat16),
            jax.ShapeDtypeStruct((rows, wide_k), jnp.bfloat16),
            jax.ShapeDtypeStruct((rows, wide_k), jnp.bfloat16),
        ],
        in_specs=whole_specs(len(parts) + 3),
        out_specs=whole_specs(4),
        compiler_params=pltpu.CompilerParams(vmem_limit_bytes=24 * 2**20),
        cost_estimate=pl.CostEstimate(
            flops=2 * slots * rows * wide_q, bytes_accessed=8 * rows * wide_q, transcendentals=0
        ),
        name="pack",
    )(*parts, cosine, sine, route)


def join_kernel(back, route, query, key, value, out):
    rows = query.shape[0]
    heads = key.shape[1] // HEAD_SIZE
    far = dot(route[...], back[...], (((0,), (0,)), ((), ())))
    stat = far[:, heads * GROUP * HEAD_SIZE :]
    row = lax.broadcasted_iota(jnp.int32, (rows, rows), 0)
    other = lax.broadcasted_iota(jnp.int32, (rows, rows), 1)
    allowed = (row // DECODE_STEPS == other // DECODE_STEPS) & (other <= row)
    for head in range(heads):
        own = slice(head * HEAD_SIZE, (head + 1) * HEAD_SIZE)
        for member in range(GROUP):
            column = head * GROUP + member
            at = slice(column * HEAD_SIZE, (column + 1) * HEAD_SIZE)
            score = jnp.where(allowed, dot(query[:, at], key[:, own], NT) * SCALE, -1e30)
            top = jnp.max(score, axis=1, keepdims=True)
            weight = jnp.exp(score - top)
            total = jnp.sum(weight, axis=1, keepdims=True)
            near = dot(weight.astype(jnp.bfloat16), value[:, own])
            level = jnp.zeros((rows, 1), jnp.float32)
            for piece in range(PIECES):
                lane = piece * heads * GROUP + column
                level = level + stat[:, lane : lane + 1]
            both = jnp.maximum(level, top)
            left = jnp.exp(level - both)
            right = jnp.exp(top - both)
            merged = (far[:, at] * left + near * right) / (left + total * right)
            out[:, at] = merged.astype(jnp.bfloat16)


def join(back, route, query, key, value):
    return pl.pallas_call(
        join_kernel,
        out_shape=jax.ShapeDtypeStruct(query.shape, jnp.bfloat16),
        in_specs=whole_specs(5),
        out_specs=whole_specs(1)[0],
        compiler_params=pltpu.CompilerParams(vmem_limit_bytes=24 * 2**20),
        cost_estimate=pl.CostEstimate(
            flops=2 * route.shape[0] * route.shape[1] * back.shape[1],
            bytes_accessed=8 * query.shape[0] * query.shape[1],
            transcendentals=0,
        ),
        name="join",
    )(back, route, query, key, value)


def inner_size(owners):
    return 4 if owners % 4 == 0 else 1


def across(block, mask, owners):
    return lax.ppermute(block, "wide", [(i, i ^ mask) for i in range(owners)])


def plane_rows(piece, owners):
    if inner_size(owners) == 1:
        return piece
    half = piece.shape[0] // 2
    upper, lower = piece[:half], piece[half:]
    upper_1 = across(upper, 1, owners)
    lower_2 = across(lower, 2, owners)
    upper_2 = across(upper, 2, owners)
    lower_1 = across(lower, 1, owners)
    upper_3 = across(upper_1, 2, owners)
    lower_3 = across(lower_2, 1, owners)
    return jnp.concatenate(
        [upper, lower, upper_1, lower_1, upper_2, lower_2, upper_3, lower_3], axis=0
    )


def line_groups(owners, inner):
    return [[i * inner + j for i in range(owners // inner)] for j in range(inner)]


def line_tokens(tokens, owners, inner, halves):
    planes = owners // inner
    rows = tokens.shape[0] * tokens.shape[1]
    flat = tokens.reshape(rows, tokens.shape[2])
    if halves == 2:
        other = lax.ppermute(flat, "narrow", [(0, 1), (1, 0)])
        first = lax.axis_index("narrow") == 0
        flat = jnp.concatenate([jnp.where(first, flat, other), jnp.where(first, other, flat)], 1)
    else:
        flat = lax.all_gather(flat, "narrow", axis=1, tiled=True)
    if planes > 1:
        parts = flat.reshape(rows, planes, -1).transpose(1, 0, 2)
        parts = lax.all_to_all(
            parts, "wide", split_axis=0, concat_axis=0, tiled=True,
            axis_index_groups=line_groups(owners, inner),
        )
        flat = parts.reshape(planes * rows, -1)
    here = lax.axis_index("wide") % inner
    split = flat.reshape(planes * rows, inner, -1)
    return jnp.concatenate(
        [lax.dynamic_index_in_dim(split, here ^ j, 1, keepdims=False) for j in range(inner)], axis=1
    )


def line_sums(partial, owners, inner):
    planes = owners // inner
    if planes == 1:
        return [partial]
    rows = partial.shape[0] // planes
    parts = lax.all_to_all(
        partial.reshape(planes, rows, -1), "wide", split_axis=0, concat_axis=0, tiled=True,
        axis_index_groups=line_groups(owners, inner),
    )
    return [parts[i] for i in range(planes)]


def exchange(block):
    return lax.all_to_all(block, "wide", split_axis=0, concat_axis=0, tiled=True)


def on_device(tokens, qkv_weight, rotated_prefix_keys, shared_prefix_values, prefix_of, positions):
    rows_dev = tokens.shape[0]
    owners = lax.axis_size("wide")
    halves = lax.axis_size("narrow")
    inner = inner_size(owners)
    rows = rows_dev * DECODE_STEPS
    capacity = max(2, (2 * rows_dev + owners - 1) // owners)
    slots = owners * capacity
    kv_local = rotated_prefix_keys.shape[2] // HEAD_SIZE
    chunks = 2 if kv_local % 2 == 0 else 1
    heads = kv_local // chunks
    columns = heads * (GROUP + 2) * HEAD_SIZE

    gathered = [
        plane_rows(qkv_weight[:, i * columns : (i + 1) * columns], owners) for i in range(chunks)
    ]
    inputs = line_tokens(tokens, owners, inner, halves)

    chosen = prefix_of[:, 0]
    hits = (chosen[:, None] == jnp.arange(owners, dtype=jnp.int32)[None, :]).astype(jnp.int32)
    rank = jnp.sum((jnp.cumsum(hits, axis=0) - hits) * hits, axis=1)
    target = chosen * capacity + rank
    dispatch = target[None, :] == jnp.arange(slots, dtype=jnp.int32)[:, None]
    limits = jnp.sum(jnp.where(dispatch, positions[None, :], 0), axis=1)
    bounds = exchange(limits.reshape(owners, capacity)).reshape(slots)
    bounds = jnp.repeat(bounds, DECODE_STEPS)[:, None]
    step = jnp.arange(DECODE_STEPS, dtype=jnp.int32)
    line = (target[:, None] * DECODE_STEPS + step[None, :]).reshape(rows)
    route = (
        line[None, :] == jnp.arange(slots * DECODE_STEPS, dtype=jnp.int32)[:, None]
    ).astype(jnp.bfloat16)

    half = HEAD_SIZE // 2
    freq = 10000.0 ** (-(jnp.arange(half, dtype=jnp.float32) * 2.0 / HEAD_SIZE))
    where = (positions[:, None] + step[None, :]).reshape(rows)
    angle = where[:, None].astype(jnp.float32) * freq
    cosine, sine = jnp.cos(angle), jnp.sin(angle)
    cosine = jnp.concatenate([cosine, cosine], axis=1)
    sine = jnp.concatenate([-sine, sine], axis=1)

    key_rows = rotated_prefix_keys[0]
    value_rows = shared_prefix_values[0]
    results = []
    for i in range(chunks):
        partial = dot(inputs, gathered[i]).astype(jnp.bfloat16)
        parts = line_sums(partial, owners, inner)
        packed, query, own_key, own_value = pack(parts, cosine, sine, route, heads)
        width = packed.shape[1]
        asked = exchange(packed.reshape(owners, capacity * DECODE_STEPS, width))
        asked = asked.reshape(slots * DECODE_STEPS, width)
        far = prefix_part(asked, bounds, key_rows, value_rows, i * heads, heads)
        back = exchange(far.reshape(owners, capacity * DECODE_STEPS, -1))
        back = back.reshape(slots * DECODE_STEPS, -1)
        results.append(join(back, route, query, own_key, own_value))
    return jnp.concatenate(results, axis=1).reshape(rows_dev, DECODE_STEPS, -1)


def solution(mesh):
    return jax.shard_map(
        on_device,
        mesh=mesh,
        in_specs=(
            P("wide", None, "narrow"),
            P("wide", "narrow"),
            P("wide", None, "narrow"),
            P("wide", None, "narrow"),
            P("wide", None),
            P("wide"),
        ),
        out_specs=P("wide", None, "narrow"),
        check_vma=False,
    )
```

time: 544 us -> 236 us (0.43)
  waiting for transfers between devices: 348 us -> 97.6 us
  matrix products: 57.9 us -> 11.4 us
  starting transfers between devices: 30.1 us -> 56.1 us
  Pallas kernels: 0 us -> 25.9 us
  other arithmetic: 26.3 us -> 1.97 us
  local copies, waits for them, and re-layouts: 65.7 us -> 41.5 us
  between operations: 13.7 us -> 0.34 us
    all_gather x2 -> x0, waiting for transfers between devices: 321 us -> none  [the longest x1 321 us: on_device(): lax.all_gather(qkv_weight, 'wide', axis=0, tiled=True)]
    dot_general x6 -> x2, matrix products: 57.9 us -> 11.4 us  [dot(): lax.dot_general(left, right, dims, preferred_element_type=jnp.float32)]
    dot_general x1 -> x0, local copies, waits for them, and re-layouts: 39 us -> none  [fold_rows(): return jnp.dot(inputs, piece, preferred_element_type=jnp.float32)]
    all_to_all x5 -> x8, waiting for transfers between devices: 26.7 us -> 63.9 us  [the longest x2 39.2 us: line_sums(): lax.all_to_all(partial.reshape(planes, rows, -1), 'wide', split_axis=0, c...]
    ppermute x0 -> x13, waiting for transfers between devices: none -> 33.7 us  [the longest x12 33.6 us: across(): return lax.ppermute(block, 'wide', [(i, i ^ mask) for i in range(owners)])]
    pallas_call x0 -> x6, Pallas kernels: none -> 25.9 us  [the longest x2 17.5 us: prefix_part(): pl.pallas_call(functools.partial(prefix_kernel, min(length, 512)), grid=(...]
    unnamed x9 -> x39, local copies, waits for them, and re-layouts: 4.35 us -> 22.3 us
    reduce_sum x3 -> x1, other arithmetic: 17.9 us -> 0.1 us  [on_device(): limits = jnp.sum(jnp.where(dispatch, positions[None, :], 0), axis=1)]
  transfers between devices with their start and end apart: 7 -> 21, of which waited for: 4 -> 11; matrix products, arithmetic and copies ran while one was open for 20% -> 19% of each run, Pallas kernels for 0% -> 10%
where the time goes in v1:
time: 236 us; the launch traced here: 235 us
  waiting for transfers between devices  97.6 us (41%)
  starting transfers between devices  56.1 us (24%)
  local copies, waits for them, and re-layouts  41.5 us (18%)
  Pallas kernels  25.9 us (11%)
  matrix products  11.4 us (5%)
    all_to_all x2, waiting for transfers between devices, line_sums(): lax.all_to_all(partial.reshape(planes, rows, -1), 'wide', split_axis=0, c...  39.2 us
    ppermute x12, waiting for transfers between devices, across(): return lax.ppermute(block, 'wide', [(i, i ^ mask) for i in range(owners)])  33.6 us
    all_to_all x5, starting transfers between devices, exchange(): lax.all_to_all(block, 'wide', split_axis=0, concat_axis=0, tiled=True)  25.6 us
    all_to_all x5, waiting for transfers between devices, exchange(): lax.all_to_all(block, 'wide', split_axis=0, concat_axis=0, tiled=True)  24.8 us
    unnamed x39, local copies, waits for them, and re-layouts  22.3 us
    pallas_call x2, Pallas kernels, prefix_part(): pl.pallas_call(functools.partial(prefix_kernel, min(length, 512)), grid=(...  17.5 us
    ppermute x12, starting transfers between devices, across(): return lax.ppermute(block, 'wide', [(i, i ^ mask) for i in range(owners)])  15.6 us
    dot_general x2, matrix products, dot(): lax.dot_general(left, right, dims, preferred_element_type=jnp.float32)  11.4 us
  transfers between devices with their start and end apart: 21, of which 11 were waited for; matrix products, arithmetic and copies ran while one was open for 19% of the time, Pallas kernels for 10%

profile of v1, /device:TPU:0, one launch (start us, length us, event | category | flops | bytes accessed | tf_op | source)
XLA Modules:
  0.0 234.8 jit_solution(3791860069253781449)
XLA Ops:
  0.0 2.2 reshape.95
  2.7 2.8 %fusion.7 = (bf16[160,1536]{1,0:T(8,128)(2,1)}, bf16[160,1536]{1,0:T(8,128)(2,1)}, bf16[160,1536]{1,0:T(8,128)(2,1)}, bf16[160,1536]{1,0:T(8,128)(2,1)}) fusion(bf16[320,3072]{1,0:T(8,128)(2,1)} %param.7), kind=kLoop, calls=%fused_computation.54 | loop fusion | bytes 3932160 | tf_op jit(solution)/shard_map/slice | solution.py:200
  5.5 2.5 %collective-permute-start.7 = (bf16[160,1536]{1,0:T(8,128)(2,1)}, bf16[160,1536]{1,0:T(8,128)(2,1)}, u32[]{:S(2)}, u32[]{:S(2)}) collective-permute-start(bf16[160,1536]{1,0:T(8,128)(2,1)} %get-tuple-element.24), channel_id=1, source_target_pairs={{0,2},{2,0},{4,6},{6,4},{8,10},{10,8},{12,14},{14,12},{16,18},{18,... | collective-permute-start | bytes 1474568 | tf_op jit(solution)/shard_map/ppermute | solution.py:193
  8.0 1.5 collective-permute-start.9
  10.1 1.4 slice_dynamic-update-slice_fusion.1
  11.5 2.0 collective-permute-start.1
  13.8 1.5 copy.22
  15.2 4.9 %all-to-all-start = ((bf16[4,128,1280]{1,2,0:T(8,128)(2,1)}), bf16[4,128,1280]{1,2,0:T(8,128)(2,1)S(1)}, u32[]{:S(2)}, u32[]{:S(2)}) async-start(bf16[4,128,1280]{1,2,0:T(8,128)(2,1)} %bitcast.1), calls=%async_computation | async-start | bytes 2621440 | tf_op jit(solution)/shard_map/all_to_all | solution.py:228
  21.3 1.5 collective-permute-start.4
  22.8 1.8 constant_dynamic-update-slice_fusion.11
  24.7 6.3 %collective-permute-done.8 = bf16[160,1536]{1,0:T(8,128)(2,1)} collective-permute-done((bf16[160,1536]{1,0:T(8,128)(2,1)}, bf16[160,1536]{1,0:T(8,128)(2,1)}, u32[]{:S(2)}, u32[]{:S(2)}) %collective-permute-start.8) | collective-permute-done | bytes 491552 | tf_op jit(solution)/shard_map/ppermute | solution.py:193
  30.9 2.0 collective-permute-start.11
  32.9 1.5 collective-permute-start.12
  34.4 1.8 constant_dynamic-update-slice_fusion.10
  36.3 1.9 constant_dynamic-update-slice_fusion.9
  38.2 1.9 constant_dynamic-update-slice_fusion.8
  40.0 13.1 %collective-permute-done.11 = bf16[160,1536]{1,0:T(8,128)(2,1)S(1)} collective-permute-done((bf16[160,1536]{1,0:T(8,128)(2,1)}, bf16[160,1536]{1,0:T(8,128)(2,1)S(1)}, u32[]{:S(2)}, u32[]{:S(2)}) %collective-permute-start.11) | collective-permute-done | bytes 491552 | tf_op jit(solution)/shard_map/ppermute | solution.py:193
  54.8 5.9 %all-to-all-start.3 = ((s32[16,1,8]{2,1,0:T(1,128)}), s32[16,1,8]{2,1,0:T(1,128)S(1)}, u32[]{:S(2)}, u32[]{:S(2)}) async-start(s32[16,1,8]{2,1,0:T(1,128)} %bitcast.16), calls=%async_computation.3 | async-start | bytes 16384 | tf_op jit(solution)/shard_map/all_to_all | solution.py:253
  60.8 6.1 %copy.23 = bf16[4,128,1280]{1,0,2:T(4,128)(2,1)S(1)} copy(bf16[4,128,1280]{1,2,0:T(8,128)(2,1)S(1)} %all-to-all-done) | data formatting | bytes 2621440 | tf_op jit(solution)/shard_map/all_to_all | solution.py:228
  67.6 5.8 %convolution_convert_fusion = bf16[512,1536]{1,0:T(8,128)(2,1)} fusion(bf16[1280,1536]{1,0:T(8,128)(2,1)} %constant_dynamic-update-slice_fusion.6, bf16[512,320]{0,1:T(8,128)(2,1)S(1)} %get-tuple-element.36, bf16[512,320]{0,1:T(8,128)(2,1)S(1)} %get-tuple-element.37, bf16[512,320]{0,1:T(8,128)(2,1)S(1)} %get-tuple-element.38, ...), kind=kOutput, calls=%fused_computation | convolution fusion | flops 2019295232 | bytes 6815744 | tf_op jit(solution)/shard_map/dot_general | solution.py:23
  73.4 5.0 %all-to-all-start.5 = ((bf16[4,128,1536]{2,1,0:T(8,128)(2,1)}), bf16[4,128,1536]{2,1,0:T(8,128)(2,1)S(1)}, u32[]{:S(2)}, u32[]{:S(2)}) async-start(bf16[4,128,1536]{2,1,0:T(8,128)(2,1)} %bitcast.21), calls=%async_computation.5 | async-start | bytes 3145728 | tf_op jit(solution)/shard_map/all_to_all | solution.py:245
  78.4 1.5 collective-permute-start.2
  79.9 1.5 collective-permute-start.3
  82.5 1.8 constant_dynamic-update-slice_fusion.5
  84.3 8.3 %collective-permute-done.2 = bf16[160,1536]{1,0:T(8,128)(2,1)S(1)} collective-permute-done((bf16[160,1536]{1,0:T(8,128)(2,1)S(1)}, bf16[160,1536]{1,0:T(8,128)(2,1)S(1)}, u32[]{:S(2)}, u32[]{:S(2)}) %collective-permute-start.2) | collective-permute-done | bytes 491552 | tf_op jit(solution)/shard_map/ppermute | solution.py:193
  95.1 1.8 constant_dynamic-update-slice_fusion.2
  96.9 5.1 %collective-permute-done.5 = bf16[160,1536]{1,0:T(8,128)(2,1)S(1)} collective-permute-done((bf16[160,1536]{1,0:T(8,128)(2,1)}, bf16[160,1536]{1,0:T(8,128)(2,1)S(1)}, u32[]{:S(2)}, u32[]{:S(2)}) %collective-permute-start.5) | collective-permute-done | bytes 491552 | tf_op jit(solution)/shard_map/ppermute | solution.py:193
  103.7 5.5 %convolution_convert_fusion.1 = bf16[512,1536]{1,0:T(8,128)(2,1)} fusion(bf16[1280,1536]{1,0:T(8,128)(2,1)} %constant_dynamic-update-slice_fusion, bf16[512,320]{0,1:T(8,128)(2,1)S(1)} %copy-done.7, bf16[512,320]{0,1:T(8,128)(2,1)S(1)} %copy-done.9, bf16[512,320]{0,1:T(8,128)(2,1)S(1)} %copy-done.11, bf16[512,320]{0,1:T(8,128)(2,1)S(1)} %get-tuple-element.35), kind=kOutput, calls=%fused_computation.1 | convolution fusion | flops 2019295232 | bytes 6815744 | tf_op jit(solution)/shard_map/dot_general | solution.py:23
  109.2 5.2 %all-to-all-done.5 = bf16[4,128,1536]{2,1,0:T(8,128)(2,1)S(1)} async-done(((bf16[4,128,1536]{2,1,0:T(8,128)(2,1)}), bf16[4,128,1536]{2,1,0:T(8,128)(2,1)S(1)}, u32[]{:S(2)}, u32[]{:S(2)}) %all-to-all-start.5) | async-done | bytes 1572896 | tf_op jit(solution)/shard_map/all_to_all | solution.py:245
  114.4 4.5 %all-to-all-start.1 = ((bf16[4,128,1536]{2,1,0:T(8,128)(2,1)}), bf16[4,128,1536]{2,1,0:T(8,128)(2,1)}, u32[]{:S(2)}, u32[]{:S(2)}) async-start(bf16[4,128,1536]{2,1,0:T(8,128)(2,1)} %bitcast.6), calls=%async_computation.1 | async-start | bytes 3145728 | tf_op jit(solution)/shard_map/all_to_all | solution.py:245
  121.2 34.0 %all-to-all-done.1 = bf16[4,128,1536]{2,1,0:T(8,128)(2,1)} async-done(((bf16[4,128,1536]{2,1,0:T(8,128)(2,1)}), bf16[4,128,1536]{2,1,0:T(8,128)(2,1)}, u32[]{:S(2)}, u32[]{:S(2)}) %all-to-all-start.1) | async-done | bytes 1572896 | tf_op jit(solution)/shard_map/all_to_all | solution.py:245
  155.2 4.6 %all-to-all-start.6 = ((bf16[16,16,1024]{2,1,0:T(8,128)(2,1)}), bf16[16,16,1024]{2,1,0:T(8,128)(2,1)S(1)}, u32[]{:S(2)}, u32[]{:S(2)}) async-start(bf16[16,16,1024]{2,1,0:T(8,128)(2,1)} %bitcast.26), calls=%async_computation.6 | async-start | bytes 1048576 | tf_op jit(solution)/shard_map/all_to_all | solution.py:253
  159.9 1.5 slice_bitcast_fusion.4
  161.4 1.3 pack.2
  162.7 10.8 %all-to-all-done.6 = bf16[16,16,1024]{2,1,0:T(8,128)(2,1)S(1)} async-done(((bf16[16,16,1024]{2,1,0:T(8,128)(2,1)}), bf16[16,16,1024]{2,1,0:T(8,128)(2,1)S(1)}, u32[]{:S(2)}, u32[]{:S(2)}) %all-to-all-start.6) | async-done | bytes 524320 | tf_op jit(solution)/shard_map/all_to_all | solution.py:253
  173.4 3.8 %all-to-all-start.2 = ((bf16[16,16,1024]{2,1,0:T(8,128)(2,1)}), bf16[16,16,1024]{2,1,0:T(8,128)(2,1)S(1)}, u32[]{:S(2)}, u32[]{:S(2)}) async-start(bf16[16,16,1024]{2,1,0:T(8,128)(2,1)} %bitcast.14), calls=%async_computation.2 | async-start | bytes 1048576 | tf_op jit(solution)/shard_map/all_to_all | solution.py:253
  178.7 1.6 copy-done
  180.3 1.6 copy-done.2
  181.9 8.7 %prefix_part.3 = bf16[256,1152]{1,0:T(8,128)(2,1)} custom-call(bf16[256,1024]{1,0:T(8,128)(2,1)S(1)} %bitcast.56, s32[256,1]{1,0:T(8,128)S(1)} %broadcast_in_dim_reshape.6.limit, bf16[2048,512]{1,0:T(8,128)(2,1)S(1)} %bitcast.58, bf16[2048,512]{1,0:T(8,128)(2,1)S(1)} %bitcast.60), custom_call_target="tpu_custom_call" | custom-call | flops 2147483648 | bytes 2097152 | tf_op jit(solution)/shard_map/prefix_part/pallas_call | solution.py:74
  190.9 6.6 %all-to-all-start.7 = ((bf16[16,16,1152]{2,1,0:T(8,128)(2,1)}), bf16[16,16,1152]{2,1,0:T(8,128)(2,1)S(1)}, u32[]{:S(2)}, u32[]{:S(2)}) async-start(bf16[16,16,1152]{2,1,0:T(8,128)(2,1)} %bitcast.28), calls=%async_computation.7 | async-start | bytes 1179648 | tf_op jit(solution)/shard_map/all_to_all | solution.py:253
  197.5 1.6 copy-done.1
  199.1 1.6 copy-done.3
  200.7 8.7 %prefix_part.2 = bf16[256,1152]{1,0:T(8,128)(2,1)} custom-call(bf16[256,1024]{1,0:T(8,128)(2,1)S(1)} %bitcast.57, s32[256,1]{1,0:T(8,128)S(1)} %broadcast_in_dim_reshape.6.limit, bf16[2048,512]{1,0:T(8,128)(2,1)S(1)} %bitcast.59, bf16[2048,512]{1,0:T(8,128)(2,1)S(1)} %bitcast.61), custom_call_target="tpu_custom_call" | custom-call | flops 2147483648 | bytes 2097152 | tf_op jit(solution)/shard_map/prefix_part/pallas_call | solution.py:74
  209.5 2.4 %all-to-all-done.7 = bf16[16,16,1152]{2,1,0:T(8,128)(2,1)S(1)} async-done(((bf16[16,16,1152]{2,1,0:T(8,128)(2,1)}), bf16[16,16,1152]{2,1,0:T(8,128)(2,1)S(1)}, u32[]{:S(2)}, u32[]{:S(2)}) %all-to-all-start.7) | async-done | bytes 589856 | tf_op jit(solution)/shard_map/all_to_all | solution.py:253
  211.8 4.5 %all-to-all-start.4 = ((bf16[16,16,1152]{2,1,0:T(8,128)(2,1)}), bf16[16,16,1152]{2,1,0:T(8,128)(2,1)S(1)}, u32[]{:S(2)}, u32[]{:S(2)}) async-start(bf16[16,16,1152]{2,1,0:T(8,128)(2,1)} %bitcast.19), calls=%async_computation.4 | async-start | bytes 1179648 | tf_op jit(solution)/shard_map/all_to_all | solution.py:253
  216.4 2.9 %join.3 = bf16[128,1024]{1,0:T(8,128)(2,1)S(1)} custom-call(bf16[256,1152]{1,0:T(8,128)(2,1)S(1)} %bitcast.54, bf16[256,128]{1,0:T(8,128)(2,1)S(1)} %fusion.refs_6_.route, bf16[128,1024]{1,0:T(8,128)(2,1)S(1)} %get-tuple-element.18.query, bf16[128,256]{1,0:T(8,128)(2,1)S(1)} %get-tuple-element.19.key, bf16[128,256]{1,0:T(8,128)(2,1)S(1)} %get-tuple-element.20.value), custom_call_target="tpu_custom_call" | custom-call | flops 75497472 | bytes 1048576 | tf_op jit(solution)/shard_map/join/pallas_call | solution.py:173
  219.3 11.3 %all-to-all-done.4 = bf16[16,16,1152]{2,1,0:T(8,128)(2,1)S(1)} async-done(((bf16[16,16,1152]{2,1,0:T(8,128)(2,1)}), bf16[16,16,1152]{2,1,0:T(8,128)(2,1)S(1)}, u32[]{:S(2)}, u32[]{:S(2)}) %all-to-all-start.4) | async-done | bytes 589856 | tf_op jit(solution)/shard_map/all_to_all | solution.py:253
  230.7 2.9 %join.2 = bf16[128,1024]{1,0:T(8,128)(2,1)S(1)} custom-call(bf16[256,1152]{1,0:T(8,128)(2,1)S(1)} %bitcast.55, bf16[256,128]{1,0:T(8,128)(2,1)S(1)} %fusion.refs_6_.route, bf16[128,1024]{1,0:T(8,128)(2,1)S(1)} %get-tuple-element.14.query, bf16[128,256]{1,0:T(8,128)(2,1)S(1)} %get-tuple-element.15.key, bf16[128,256]{1,0:T(8,128)(2,1)S(1)} %get-tuple-element.16.value), custom_call_target="tpu_custom_call" | custom-call | flops 75497472 | bytes 1048576 | tf_op jit(solution)/shard_map/join/pallas_call | solution.py:173
  (75 shorter events, 15.2 us)
Async XLA Ops:
  0.0 10.1 %copy-start.4 = (bf16[320,3072]{1,0:T(8,128)(2,1)S(1)}, bf16[320,3072]{1,0:T(8,128)(2,1)}, u32[]{:S(2)}) copy-start(bf16[320,3072]{1,0:T(8,128)(2,1)} %param.7) | copy-start | bytes 5898244
  2.2 9.3 %collective-permute-start = (bf16[128,2560]{1,0:T(8,128)(2,1)S(1)}, bf16[128,2560]{1,0:T(8,128)(2,1)S(1)}, u32[]{:S(2)}, u32[]{:S(2)}) collective-permute-start(bf16[128,2560]{1,0:T(8,128)(2,1)S(1)} %reshape.95), channel_id=1, source_target_pairs={{0,1},{1,0},{2,3},{3,2},{4,5},{5,4},{6,7},{7,6},{8,9},{9,8},{10,11... | collective-permute-start | bytes 1966088 | tf_op jit(solution)/shard_map/ppermute | solution.py:221
  5.5 15.8 %collective-permute-start.7 = (bf16[160,1536]{1,0:T(8,128)(2,1)}, bf16[160,1536]{1,0:T(8,128)(2,1)}, u32[]{:S(2)}, u32[]{:S(2)}) collective-permute-start(bf16[160,1536]{1,0:T(8,128)(2,1)} %get-tuple-element.24), channel_id=1, source_target_pairs={{0,2},{2,0},{4,6},{6,4},{8,10},{10,8},{12,14},{14,12},{16,18},{18,... | collective-permute-start | bytes 1474568 | tf_op jit(solution)/shard_map/ppermute | solution.py:193
  8.0 28.2 %collective-permute-start.9 = (bf16[160,1536]{1,0:T(8,128)(2,1)}, bf16[160,1536]{1,0:T(8,128)(2,1)}, u32[]{:S(2)}, u32[]{:S(2)}) collective-permute-start(bf16[160,1536]{1,0:T(8,128)(2,1)} %get-tuple-element.24), channel_id=1, source_target_pairs={{0,4},{2,6},{4,0},{6,2},{8,12},{10,14},{12,8},{14,10},{16,20},{18,... | collective-permute-start | bytes 1474568 | tf_op jit(solution)/shard_map/ppermute | solution.py:193
  9.5 21.4 %collective-permute-start.8 = (bf16[160,1536]{1,0:T(8,128)(2,1)}, bf16[160,1536]{1,0:T(8,128)(2,1)}, u32[]{:S(2)}, u32[]{:S(2)}) collective-permute-start(bf16[160,1536]{1,0:T(8,128)(2,1)} %get-tuple-element.23), channel_id=1, source_target_pairs={{0,2},{2,0},{4,6},{6,4},{8,10},{10,8},{12,14},{14,12},{16,18},{18,... | collective-permute-start | bytes 1474568 | tf_op jit(solution)/shard_map/ppermute | solution.py:193
  10.1 22.9 %collective-permute-start.10 = (bf16[160,1536]{1,0:T(8,128)(2,1)}, bf16[160,1536]{1,0:T(8,128)(2,1)}, u32[]{:S(2)}, u32[]{:S(2)}) collective-permute-start(bf16[160,1536]{1,0:T(8,128)(2,1)} %get-tuple-element.23), channel_id=1, source_target_pairs={{0,4},{2,6},{4,0},{6,2},{8,12},{10,14},{12,8},{14,10},{16,20},{18,... | collective-permute-start | bytes 1474568 | tf_op jit(solution)/shard_map/ppermute | solution.py:193
  11.5 69.8 %collective-permute-start.1 = (bf16[160,1536]{1,0:T(8,128)(2,1)}, bf16[160,1536]{1,0:T(8,128)(2,1)}, u32[]{:S(2)}, u32[]{:S(2)}) collective-permute-start(bf16[160,1536]{1,0:T(8,128)(2,1)} %get-tuple-element.22), channel_id=1, source_target_pairs={{0,2},{2,0},{4,6},{6,4},{8,10},{10,8},{12,14},{14,12},{16,18},{18,... | collective-permute-start | bytes 1474568 | tf_op jit(solution)/shard_map/ppermute | solution.py:193
  13.7 6.4 %copy-start.12 = (s32[64,1]{0,1:T(1,128)S(1)}, s32[64,1]{0,1:T(1,128)}, u32[]{:S(2)}) copy-start(s32[64,1]{0,1:T(1,128)} %param.10) | copy-start | bytes 772
  13.8 6.7 %copy-start.13 = (s32[64]{0:T(128)S(1)}, s32[64]{0:T(128)}, u32[]{:S(2)}) copy-start(s32[64]{0:T(128)} %param.11) | copy-start | bytes 772
  13.8 7.5 %copy-start.5 = (bf16[160,1536]{1,0:T(8,128)(2,1)S(1)}, bf16[160,1536]{1,0:T(8,128)(2,1)}, u32[]{:S(2)}) copy-start(bf16[160,1536]{1,0:T(8,128)(2,1)} %get-tuple-element.21) | copy-start | bytes 1474564
  15.2 39.6 %all-to-all-start = ((bf16[4,128,1280]{1,2,0:T(8,128)(2,1)}), bf16[4,128,1280]{1,2,0:T(8,128)(2,1)S(1)}, u32[]{:S(2)}, u32[]{:S(2)}) async-start(bf16[4,128,1280]{1,2,0:T(8,128)(2,1)} %bitcast.1), calls=%async_computation | async-start | bytes 2621440 | tf_op jit(solution)/shard_map/all_to_all | solution.py:228
  21.3 60.6 %collective-permute-start.4 = (bf16[160,1536]{1,0:T(8,128)(2,1)S(1)}, bf16[160,1536]{1,0:T(8,128)(2,1)}, u32[]{:S(2)}, u32[]{:S(2)}) collective-permute-start(bf16[160,1536]{1,0:T(8,128)(2,1)S(1)} %copy-done.5), channel_id=1, source_target_pairs={{0,4},{2,6},{4,0},{6,2},{8,12},{10,14},{12,8},{14,10},{16,20},{18,... | collective-permute-start | bytes 1474568 | tf_op jit(solution)/shard_map/ppermute | solution.py:193
  30.9 22.2 %collective-permute-start.11 = (bf16[160,1536]{1,0:T(8,128)(2,1)}, bf16[160,1536]{1,0:T(8,128)(2,1)S(1)}, u32[]{:S(2)}, u32[]{:S(2)}) collective-permute-start(bf16[160,1536]{1,0:T(8,128)(2,1)} %collective-permute-done.7), channel_id=1, source_target_pairs={{0,4},{2,6},{4,0},{6,2},{8,12},{10,14},{12,8},{14,10},{16,20},{18,... | collective-permute-start | bytes 1474568 | tf_op jit(solution)/shard_map/ppermute | solution.py:193
  32.9 21.1 %collective-permute-start.12 = (bf16[160,1536]{1,0:T(8,128)(2,1)}, bf16[160,1536]{1,0:T(8,128)(2,1)S(1)}, u32[]{:S(2)}, u32[]{:S(2)}) collective-permute-start(bf16[160,1536]{1,0:T(8,128)(2,1)} %collective-permute-done.10), channel_id=1, source_target_pairs={{0,2},{2,0},{4,6},{6,4},{8,10},{10,8},{12,14},{14,12},{16,18},{18,... | collective-permute-start | bytes 1474568 | tf_op jit(solution)/shard_map/ppermute | solution.py:193
  54.8 18.6 %all-to-all-start.3 = ((s32[16,1,8]{2,1,0:T(1,128)}), s32[16,1,8]{2,1,0:T(1,128)S(1)}, u32[]{:S(2)}, u32[]{:S(2)}) async-start(s32[16,1,8]{2,1,0:T(1,128)} %bitcast.16), calls=%async_computation.3 | async-start | bytes 16384 | tf_op jit(solution)/shard_map/all_to_all | solution.py:253
  67.6 5.9 %copy-start.6 = (bf16[512,320]{0,1:T(8,128)(2,1)}, bf16[512,320]{0,1:T(8,128)(2,1)S(1)}, u32[]{:S(2)}) copy-start(bf16[512,320]{0,1:T(8,128)(2,1)S(1)} %get-tuple-element.36) | copy-start | bytes 983044
  67.6 5.8 %copy-start.8 = (bf16[512,320]{0,1:T(8,128)(2,1)}, bf16[512,320]{0,1:T(8,128)(2,1)S(1)}, u32[]{:S(2)}) copy-start(bf16[512,320]{0,1:T(8,128)(2,1)S(1)} %get-tuple-element.37) | copy-start | bytes 983044
  67.6 5.8 %copy-start.10 = (bf16[512,320]{0,1:T(8,128)(2,1)}, bf16[512,320]{0,1:T(8,128)(2,1)S(1)}, u32[]{:S(2)}) copy-start(bf16[512,320]{0,1:T(8,128)(2,1)S(1)} %get-tuple-element.38) | copy-start | bytes 983044
  73.4 40.9 %all-to-all-start.5 = ((bf16[4,128,1536]{2,1,0:T(8,128)(2,1)}), bf16[4,128,1536]{2,1,0:T(8,128)(2,1)S(1)}, u32[]{:S(2)}, u32[]{:S(2)}) async-start(bf16[4,128,1536]{2,1,0:T(8,128)(2,1)} %bitcast.21), calls=%async_computation.5 | async-start | bytes 3145728 | tf_op jit(solution)/shard_map/all_to_all | solution.py:245
  78.4 14.2 %collective-permute-start.2 = (bf16[160,1536]{1,0:T(8,128)(2,1)S(1)}, bf16[160,1536]{1,0:T(8,128)(2,1)S(1)}, u32[]{:S(2)}, u32[]{:S(2)}) collective-permute-start(bf16[160,1536]{1,0:T(8,128)(2,1)S(1)} %copy-done.5), channel_id=1, source_target_pairs={{0,2},{2,0},{4,6},{6,4},{8,10},{10,8},{12,14},{14,12},{16,18},{18,... | collective-permute-start | bytes 1474568 | tf_op jit(solution)/shard_map/ppermute | solution.py:193
  79.9 14.4 %collective-permute-start.3 = (bf16[160,1536]{1,0:T(8,128)(2,1)}, bf16[160,1536]{1,0:T(8,128)(2,1)S(1)}, u32[]{:S(2)}, u32[]{:S(2)}) collective-permute-start(bf16[160,1536]{1,0:T(8,128)(2,1)} %get-tuple-element.22), channel_id=1, source_target_pairs={{0,4},{2,6},{4,0},{6,2},{8,12},{10,14},{12,8},{14,10},{16,20},{18,... | collective-permute-start | bytes 1474568 | tf_op jit(solution)/shard_map/ppermute | solution.py:193
  81.4 20.7 %collective-permute-start.5 = (bf16[160,1536]{1,0:T(8,128)(2,1)}, bf16[160,1536]{1,0:T(8,128)(2,1)S(1)}, u32[]{:S(2)}, u32[]{:S(2)}) collective-permute-start(bf16[160,1536]{1,0:T(8,128)(2,1)} %collective-permute-done.1), channel_id=1, source_target_pairs={{0,4},{2,6},{4,0},{6,2},{8,12},{10,14},{12,8},{14,10},{16,20},{18,... | collective-permute-start | bytes 1474568 | tf_op jit(solution)/shard_map/ppermute | solution.py:193
  81.9 20.9 %collective-permute-start.6 = (bf16[160,1536]{1,0:T(8,128)(2,1)}, bf16[160,1536]{1,0:T(8,128)(2,1)S(1)}, u32[]{:S(2)}, u32[]{:S(2)}) collective-permute-start(bf16[160,1536]{1,0:T(8,128)(2,1)} %collective-permute-done.4), channel_id=1, source_target_pairs={{0,2},{2,0},{4,6},{6,4},{8,10},{10,8},{12,14},{14,12},{16,18},{18,... | collective-permute-start | bytes 1474568 | tf_op jit(solution)/shard_map/ppermute | solution.py:193
  84.3 19.3 %copy-start.7 = (bf16[512,320]{0,1:T(8,128)(2,1)S(1)}, bf16[512,320]{0,1:T(8,128)(2,1)}, u32[]{:S(2)}) copy-start(bf16[512,320]{0,1:T(8,128)(2,1)} %copy-done.6) | copy-start | bytes 983044
  84.3 19.3 %copy-start.9 = (bf16[512,320]{0,1:T(8,128)(2,1)S(1)}, bf16[512,320]{0,1:T(8,128)(2,1)}, u32[]{:S(2)}) copy-start(bf16[512,320]{0,1:T(8,128)(2,1)} %copy-done.8) | copy-start | bytes 983044
  84.3 19.3 %copy-start.11 = (bf16[512,320]{0,1:T(8,128)(2,1)S(1)}, bf16[512,320]{0,1:T(8,128)(2,1)}, u32[]{:S(2)}) copy-start(bf16[512,320]{0,1:T(8,128)(2,1)} %copy-done.10) | copy-start | bytes 983044
  114.4 40.9 %all-to-all-start.1 = ((bf16[4,128,1536]{2,1,0:T(8,128)(2,1)}), bf16[4,128,1536]{2,1,0:T(8,128)(2,1)}, u32[]{:S(2)}, u32[]{:S(2)}) async-start(bf16[4,128,1536]{2,1,0:T(8,128)(2,1)} %bitcast.6), calls=%async_computation.1 | async-start | bytes 3145728 | tf_op jit(solution)/shard_map/all_to_all | solution.py:245
  155.2 18.2 %all-to-all-start.6 = ((bf16[16,16,1024]{2,1,0:T(8,128)(2,1)}), bf16[16,16,1024]{2,1,0:T(8,128)(2,1)S(1)}, u32[]{:S(2)}, u32[]{:S(2)}) async-start(bf16[16,16,1024]{2,1,0:T(8,128)(2,1)} %bitcast.26), calls=%async_computation.6 | async-start | bytes 1048576 | tf_op jit(solution)/shard_map/all_to_all | solution.py:253
  173.4 17.4 %all-to-all-start.2 = ((bf16[16,16,1024]{2,1,0:T(8,128)(2,1)}), bf16[16,16,1024]{2,1,0:T(8,128)(2,1)S(1)}, u32[]{:S(2)}, u32[]{:S(2)}) async-start(bf16[16,16,1024]{2,1,0:T(8,128)(2,1)} %bitcast.14), calls=%async_computation.2 | async-start | bytes 1048576 | tf_op jit(solution)/shard_map/all_to_all | solution.py:253
  178.7 1.6 copy-start
  180.3 1.6 copy-start.2
  190.9 21.0 %all-to-all-start.7 = ((bf16[16,16,1152]{2,1,0:T(8,128)(2,1)}), bf16[16,16,1152]{2,1,0:T(8,128)(2,1)S(1)}, u32[]{:S(2)}, u32[]{:S(2)}) async-start(bf16[16,16,1152]{2,1,0:T(8,128)(2,1)} %bitcast.28), calls=%async_computation.7 | async-start | bytes 1179648 | tf_op jit(solution)/shard_map/all_to_all | solution.py:253
  197.5 1.6 copy-start.1
  199.1 1.6 copy-start.3
  211.8 18.8 %all-to-all-start.4 = ((bf16[16,16,1152]{2,1,0:T(8,128)(2,1)}), bf16[16,16,1152]{2,1,0:T(8,128)(2,1)S(1)}, u32[]{:S(2)}, u32[]{:S(2)}) async-start(bf16[16,16,1152]{2,1,0:T(8,128)(2,1)} %bitcast.19), calls=%async_computation.4 | async-start | bytes 1179648 | tf_op jit(solution)/shard_map/all_to_all | solution.py:253

commit v2 on v1

v2 whole, which is shorter than its diff:
```python
import functools

import jax
import jax.numpy as jnp
from jax import lax
from jax.experimental import pallas as pl
from jax.experimental.pallas import tpu as pltpu
from jax.sharding import PartitionSpec as P

QUERY_HEADS = 32
KEY_VALUE_HEADS = 8
HEAD_SIZE = 128
DECODE_STEPS = 2
GROUP = QUERY_HEADS // KEY_VALUE_HEADS
SCALE = 1.0 / HEAD_SIZE**0.5
LOG2E = 1.4426950408889634
FLOOR = 512
RS = ("relay2", "relay2")
FARGATE = True
P2GATE = False
PROJ_MB = 40
TINY0 = True
TINY1 = False
SETTLE = 20000000
KP = 1.0
KA = 1.0
PGATE = False
KVLATE = False
CHUNKS = (2, 2)
PIECES = 3
NT = (((1,), (1,)), ((), ()))
NN = (((1,), (0,)), ((), ()))


def dot(left, right, dims=NN):
    return lax.dot_general(left, right, dims, preferred_element_type=jnp.float32)


def whole_specs(count):
    return [pl.BlockSpec(memory_space=pltpu.VMEM)] * count


def prefix_kernel(tile, heads, asked, marks, keys, values, out):
    rows = asked.shape[0]
    length = keys.shape[0]
    head = pl.program_id(0)
    wide = heads * GROUP * HEAD_SIZE
    bound = (marks[:, 0:1].astype(jnp.float32) + marks[:, 1:2].astype(jnp.float32)).astype(jnp.int32)
    lane = lax.broadcasted_iota(jnp.int32, (rows, HEAD_SIZE), 1)

    @pl.when(head == 0)
    def _():
        out[:, wide:] = jnp.zeros((rows, HEAD_SIZE), out.dtype)

    stat = out[:, wide:].astype(jnp.float32)
    ones = jnp.ones((tile, HEAD_SIZE), jnp.bfloat16)
    for member in range(GROUP):
        column = head * GROUP + member
        at = pl.ds(pl.multiple_of(column * HEAD_SIZE, HEAD_SIZE), HEAD_SIZE)
        query = asked[:, at]
        parts = []
        top = None
        for start in range(0, length, tile):
            score = dot(query, keys[start : start + tile, :], NT)
            if start + tile > FLOOR:
                where = start + lax.broadcasted_iota(jnp.int32, score.shape, 1)
                score = jnp.where(where < bound, score, -1e30)
            parts.append(score)
            high = jnp.max(score, axis=1, keepdims=True)
            top = high if top is None else jnp.maximum(top, high)
        total = jnp.zeros((rows, 1), jnp.float32)
        summed = jnp.zeros((rows, HEAD_SIZE), jnp.float32)
        for index, start in enumerate(range(0, length, tile)):
            weight = jnp.exp2((parts[index] - top) * (SCALE * LOG2E)).astype(jnp.bfloat16)
            both = dot(weight, jnp.concatenate([values[start : start + tile, :], ones], axis=1))
            summed = summed + both[:, :HEAD_SIZE]
            total = total + both[:, HEAD_SIZE : HEAD_SIZE + 1]
        out[:, at] = (summed / total).astype(jnp.bfloat16)
        left = top * SCALE + jnp.log(total)
        for piece in range(PIECES):
            part = left.astype(jnp.bfloat16).astype(jnp.float32)
            stat = jnp.where(lane == piece * heads * GROUP + column, part, stat)
            left = left - part
    out[:, wide:] = stat.astype(jnp.bfloat16)


def prefix_part(asked, marks, keys, values, first, heads):
    rows = asked.shape[0]
    length = keys.shape[0]
    wide = heads * GROUP * HEAD_SIZE
    last = marks.shape[1] // HEAD_SIZE - 1
    block = pl.BlockSpec((length, HEAD_SIZE), lambda i: (0, first + i))
    return pl.pallas_call(
        functools.partial(prefix_kernel, min(length, 512), heads),
        grid=(heads,),
        out_shape=jax.ShapeDtypeStruct((rows, wide + HEAD_SIZE), jnp.bfloat16),
        in_specs=[
            pl.BlockSpec((rows, wide), lambda i: (0, 0)),
            pl.BlockSpec((rows, HEAD_SIZE), lambda i: (0, last)),
            block,
            block,
        ],
        out_specs=pl.BlockSpec((rows, wide + HEAD_SIZE), lambda i: (0, 0)),
        compiler_params=pltpu.CompilerParams(vmem_limit_bytes=56 * 2**20),
        cost_estimate=pl.CostEstimate(
            flops=int(KA * 4 * rows * length * wide),
            bytes_accessed=4 * length * heads * HEAD_SIZE,
            transcendentals=rows * length * heads * GROUP,
        ),
        name="prefix_part",
    )(asked, marks, keys, values)


def pack_kernel(count, *refs):
    parts, (cosine, sine, route, marks, asked, query, key, value) = refs[:count], refs[count:]
    heads = key.shape[1] // HEAD_SIZE

    def column(index):
        at = slice(index * HEAD_SIZE, (index + 1) * HEAD_SIZE)
        total = parts[0][:, at].astype(jnp.float32)
        for part in parts[1:]:
            total = total + part[:, at].astype(jnp.float32)
        return total

    def rotated(block):
        turned = pltpu.roll(block, HEAD_SIZE // 2, 1)
        return (block * cosine[...] + turned * sine[...]).astype(jnp.bfloat16)

    for head in range(heads):
        base = head * (GROUP + 2)
        for member in range(GROUP):
            at = head * GROUP + member
            query[:, at * HEAD_SIZE : (at + 1) * HEAD_SIZE] = rotated(column(base + member))
        at = slice(head * HEAD_SIZE, (head + 1) * HEAD_SIZE)
        key[:, at] = rotated(column(base + GROUP))
        value[:, at] = column(base + GROUP + 1).astype(jnp.bfloat16)
    wide = query.shape[1]
    asked[:, :wide] = dot(route[...], query[...]).astype(jnp.bfloat16)
    if asked.shape[1] > wide:
        asked[:, wide:] = dot(route[...], marks[...]).astype(jnp.bfloat16)


def pack(parts, cosine, sine, route, marks, heads, marked):
    rows = cosine.shape[0]
    slots = route.shape[0]
    wide_q, wide_k = heads * GROUP * HEAD_SIZE, heads * HEAD_SIZE
    return pl.pallas_call(
        functools.partial(pack_kernel, len(parts)),
        out_shape=[
            jax.ShapeDtypeStruct((slots, wide_q + marked * HEAD_SIZE), jnp.bfloat16),
            jax.ShapeDtypeStruct((rows, wide_q), jnp.bfloat16),
            jax.ShapeDtypeStruct((rows, wide_k), jnp.bfloat16),
            jax.ShapeDtypeStruct((rows, wide_k), jnp.bfloat16),
        ],
        in_specs=whole_specs(len(parts) + 4),
        out_specs=whole_specs(4),
        compiler_params=pltpu.CompilerParams(vmem_limit_bytes=24 * 2**20),
        cost_estimate=pl.CostEstimate(
            flops=2 * slots * rows * wide_q, bytes_accessed=8 * rows * wide_q, transcendentals=0
        ),
        name="pack",
    )(*parts, cosine, sine, route, marks)


def near_kernel(query, key, value, summed, stat):
    rows = query.shape[0]
    heads = key.shape[1] // HEAD_SIZE
    lane = lax.broadcasted_iota(jnp.int32, (rows, HEAD_SIZE), 1)
    kept = jnp.zeros((rows, HEAD_SIZE), jnp.float32)
    row = lax.broadcasted_iota(jnp.int32, (rows, rows), 0)
    other = lax.broadcasted_iota(jnp.int32, (rows, rows), 1)
    allowed = (row // DECODE_STEPS == other // DECODE_STEPS) & (other <= row)
    for head in range(heads):
        own = slice(head * HEAD_SIZE, (head + 1) * HEAD_SIZE)
        for member in range(GROUP):
            column = head * GROUP + member
            at = slice(column * HEAD_SIZE, (column + 1) * HEAD_SIZE)
            score = jnp.where(allowed, dot(query[:, at], key[:, own], NT) * SCALE, -1e30)
            top = jnp.max(score, axis=1, keepdims=True)
            weight = jnp.exp(score - top)
            total = jnp.sum(weight, axis=1, keepdims=True)
            summed[:, at] = dot(weight.astype(jnp.bfloat16), value[:, own])
            kept = jnp.where(lane == column, top, kept)
            kept = jnp.where(lane == heads * GROUP + column, total, kept)
    stat[...] = kept


def near_part(query, key, value):
    rows, wide = query.shape
    return pl.pallas_call(
        near_kernel,
        out_shape=[
            jax.ShapeDtypeStruct((rows, wide), jnp.float32),
            jax.ShapeDtypeStruct((rows, HEAD_SIZE), jnp.float32),
        ],
        in_specs=whole_specs(3),
        out_specs=whole_specs(2),
        compiler_params=pltpu.CompilerParams(vmem_limit_bytes=24 * 2**20),
        cost_estimate=pl.CostEstimate(
            flops=4 * rows * rows * wide, bytes_accessed=8 * rows * wide, transcendentals=0
        ),
        name="near_part",
    )(query, key, value)


def join_kernel(back, route, summed, stat, out):
    wide = summed.shape[1]
    columns = wide // HEAD_SIZE
    far = dot(route[...], back[...], (((0,), (0,)), ((), ())))
    marks = far[:, wide:]
    for column in range(columns):
        at = slice(column * HEAD_SIZE, (column + 1) * HEAD_SIZE)
        level = marks[:, column : column + 1]
        for piece in range(1, PIECES):
            lane = piece * columns + column
            level = level + marks[:, lane : lane + 1]
        top = stat[:, column : column + 1]
        total = stat[:, columns + column : columns + column + 1]
        both = jnp.maximum(level, top)
        left = jnp.exp(level - both)
        right = jnp.exp(top - both)
        merged = (far[:, at] * left + summed[:, at] * right) / (left + total * right)
        out[:, at] = merged.astype(jnp.bfloat16)


def join(back, route, summed, stat):
    return pl.pallas_call(
        join_kernel,
        out_shape=jax.ShapeDtypeStruct(summed.shape, jnp.bfloat16),
        in_specs=whole_specs(4),
        out_specs=whole_specs(1)[0],
        compiler_params=pltpu.CompilerParams(vmem_limit_bytes=24 * 2**20),
        cost_estimate=pl.CostEstimate(
            flops=2 * route.shape[0] * route.shape[1] * back.shape[1],
            bytes_accessed=8 * summed.shape[0] * summed.shape[1],
            transcendentals=0,
        ),
        name="join",
    )(back, route, summed, stat)


def project_kernel(index, *refs):
    pieces, mine, other, outs, (rows, weight) = (
        refs[:8], refs[8:12], refs[12:16], refs[-6:-2], refs[-2:]
    )
    half, columns = pieces[0].shape
    size = mine[0].shape[0]
    place, end, holder = index[0], index[1], index[2]
    for i, piece in enumerate(pieces):
        start = (place ^ (i // 2)) * (2 * half) + (i % 2) * half
        weight[pl.ds(pl.multiple_of(start, 16), half), :] = piece[...]

    def fill(source):
        rows[:size] = source[0][...]
        rows[3 * size :] = source[2][...]

        @pl.when(end == 1)
        def _():
            rows[size : 2 * size] = source[3][...]
            rows[2 * size : 3 * size] = source[1][...]

        @pl.when(end == 0)
        def _():
            rows[size : 2 * size] = source[1][...]
            rows[2 * size : 3 * size] = source[3][...]

    @pl.when(holder == 1)
    def _():
        fill(mine)

    @pl.when(holder == 0)
    def _():
        fill(other)

    tile = 256
    for start in range(0, columns, tile):
        result = dot(rows[...], weight[:, start : start + tile]).astype(jnp.bfloat16)
        for i, out in enumerate(outs):
            out[:, start : start + tile] = result[i * size : (i + 1) * size]


def settle_kernel(*refs):
    refs[-1][...] = jnp.zeros_like(refs[-1])


def settle(arrived, size):
    return pl.pallas_call(
        settle_kernel,
        out_shape=jax.ShapeDtypeStruct((8, HEAD_SIZE), jnp.float32),
        in_specs=[pl.BlockSpec(memory_space=pl.ANY)] * len(arrived),
        out_specs=pl.BlockSpec(memory_space=pltpu.VMEM),
        cost_estimate=pl.CostEstimate(flops=0, bytes_accessed=size, transcendentals=0),
        name="settle",
    )(*arrived)


def project(index, pieces, mine, other, marks):
    columns = pieces[0].shape[1]
    size, depth = mine[0].shape
    return pl.pallas_call(
        project_kernel,
        out_shape=[jax.ShapeDtypeStruct((size, columns), jnp.bfloat16)] * 4,
        in_specs=[pl.BlockSpec(memory_space=pltpu.SMEM)]
        + whole_specs(16)
        + [pl.BlockSpec(memory_space=pl.ANY)] * len(marks),
        out_specs=whole_specs(4),
        scratch_shapes=[
            pltpu.VMEM((4 * size, depth), jnp.bfloat16),
            pltpu.VMEM((depth, columns), jnp.bfloat16),
        ],
        compiler_params=pltpu.CompilerParams(vmem_limit_bytes=PROJ_MB * 2**20),
        cost_estimate=pl.CostEstimate(
            flops=int(KP * 8 * size * depth * columns), bytes_accessed=2 * depth * columns, transcendentals=0
        ),
        name="project",
    )(index, *pieces, *mine, *other, *marks)


def after(value, *done):
    return lax.optimization_barrier((value, *done))[0]


def passed_on(source):
    return lax.ppermute(source[:16, :HEAD_SIZE], "narrow", [(0, 1), (1, 0)])[:1, :1]


def behind(value, mark):
    return jnp.where(mark == mark, value, 0).astype(value.dtype)


def inner_size(owners):
    return 4 if owners % 4 == 0 else 1


def across(block, mask, owners):
    return lax.ppermute(block, "wide", [(i, i ^ mask) for i in range(owners)])


def first_round(piece, owners, gate):
    half = piece.shape[0] // 2
    upper, lower = piece[:half], piece[half:]
    if gate is not None:
        upper, lower = after((upper, lower), *gate)
    return [upper, lower, across(upper, 1, owners), across(lower, 2, owners)]


def second_round(blocks, owners):
    upper, lower, upper_1, lower_2 = lax.optimization_barrier(blocks) if P2GATE else blocks
    upper_2, lower_1 = across(upper, 2, owners), across(lower, 1, owners)
    upper_3, lower_3 = across(upper_1, 2, owners), across(lower_2, 1, owners)
    return [upper, lower, upper_1, lower_1, upper_2, lower_2, upper_3, lower_3]


def line_groups(owners, inner):
    return [[i * inner + j for i in range(owners // inner)] for j in range(inner)]


def line_tokens(tokens, owners, inner, gate):
    plane = lax.axis_index("wide") // inner
    rows = tokens.shape[0] * tokens.shape[1]
    flat = tokens.reshape(rows, tokens.shape[2])
    if gate is not None:
        flat = behind(flat, gate)
    width = flat.shape[1] // 2
    even = plane % 2 == 0
    same = jnp.where(even, flat[:, :width], flat[:, width:])
    swap = jnp.where(even, flat[:, width:], flat[:, :width])
    blocks = [same]
    for mask, block in ((1, swap), (2, same), (3, swap)):
        pairs = []
        for owner in range(owners):
            there = owner ^ (mask * inner)
            core = there // inner // 2
            pairs.append((owner * 2 + core, there * 2 + core))
        blocks.append(lax.ppermute(block, ("wide", "narrow"), pairs))
    return blocks


def from_other_core(blocks):
    return [lax.ppermute(block, "narrow", [(0, 1), (1, 0)]) for block in blocks]


def line_sums(partial, owners, inner, how):
    own, first, second, third = partial
    plane = lax.axis_index("wide") // inner
    end = (plane == 0) | (plane == 3)

    def along(block, hops):
        pairs = [(a * inner + j, b * inner + j) for a, b in hops for j in range(inner)]
        return lax.ppermute(block, "wide", pairs)

    if how == "direct":
        near = along(first, [(0, 1), (1, 0), (2, 3), (3, 2)])
        mid = along(second, [(0, 3), (3, 0), (1, 2), (2, 1)])
        far = along(third, [(0, 2), (2, 0), (1, 3), (3, 1)])
        return [own, near, mid, far]
    near = along(first, [(0, 1), (1, 0), (2, 3), (3, 2)])
    middle = along(second, [(1, 2), (2, 1)])
    if how == "relay2":
        near, middle, second = lax.optimization_barrier((near, middle, second))
    outer = along(second, [(0, 1), (3, 2)])
    passed = jnp.where(end, 0, near.astype(jnp.float32))
    third = (third.astype(jnp.float32) + passed).astype(jnp.bfloat16)
    far = along(third, [(0, 2), (2, 0), (1, 3), (3, 1)])
    near = jnp.where(end, near, 0)
    return [own, near, outer, middle, far]


def project_any(tokens, qkv_weight, owners, inner):
    planes = owners // inner
    rows = tokens.shape[0] * tokens.shape[1]
    flat = lax.all_gather(tokens.reshape(rows, -1), "narrow", axis=1, tiled=True)
    weight = qkv_weight
    if inner > 1:
        groups = [[i * inner + j for j in range(inner)] for i in range(planes)]
        weight = lax.all_gather(weight, "wide", axis=0, tiled=True, axis_index_groups=groups)
    if planes == 1:
        return [dot(flat, weight)]
    lines = line_groups(owners, inner)
    parts = flat.reshape(rows, planes, -1).transpose(1, 0, 2)
    parts = lax.all_to_all(
        parts, "wide", split_axis=0, concat_axis=0, tiled=True, axis_index_groups=lines
    )
    partial = dot(parts.reshape(planes * rows, -1), weight).astype(jnp.bfloat16)
    parts = lax.all_to_all(
        partial.reshape(planes, rows, -1), "wide", split_axis=0, concat_axis=0, tiled=True,
        axis_index_groups=lines,
    )
    return [parts[i] for i in range(planes)]


def exchange(block):
    return lax.all_to_all(block, "wide", split_axis=0, concat_axis=0, tiled=True)


def on_device(tokens, qkv_weight, rotated_prefix_keys, shared_prefix_values, prefix_of, positions):
    rows_dev = tokens.shape[0]
    owners = lax.axis_size("wide")
    halves = lax.axis_size("narrow")
    inner = inner_size(owners)
    rows = rows_dev * DECODE_STEPS
    capacity = max(2, (2 * rows_dev + owners - 1) // owners)
    slots = owners * capacity
    kv_local = rotated_prefix_keys.shape[2] // HEAD_SIZE
    chunks = CHUNKS if sum(CHUNKS) == kv_local else (kv_local,)
    firsts = [sum(chunks[:i]) for i in range(len(chunks))]
    unit = (GROUP + 2) * HEAD_SIZE
    here = lax.axis_index("wide")
    plane = here // inner
    staged = owners == 4 * inner and inner == 4 and halves == 2

    if staged:
        def weight_columns(i):
            return qkv_weight[:, firsts[i] * unit : (firsts[i] + chunks[i]) * unit]

        started = first_round(weight_columns(0), owners, None)
        mine = line_tokens(tokens, owners, inner, passed_on(started[0]) if TINY0 else None)
        weights, other = second_round(started, owners), from_other_core(mine)
        index = jnp.stack(
            [
                here % inner,
                ((plane == 0) | (plane == 3)).astype(jnp.int32),
                (lax.axis_index("narrow") == plane // 2).astype(jnp.int32),
            ]
        ).astype(jnp.int32)

    chosen = prefix_of[:, 0]
    hits = (chosen[:, None] == jnp.arange(owners, dtype=jnp.int32)[None, :]).astype(jnp.int32)
    rank = jnp.sum((jnp.cumsum(hits, axis=0) - hits) * hits, axis=1)
    target = chosen * capacity + rank
    step = jnp.arange(DECODE_STEPS, dtype=jnp.int32)
    line = (target[:, None] * DECODE_STEPS + step[None, :]).reshape(rows)
    route = (
        line[None, :] == jnp.arange(slots * DECODE_STEPS, dtype=jnp.int32)[:, None]
    ).astype(jnp.bfloat16)

    count = jnp.repeat(positions, DECODE_STEPS)
    marks = jnp.stack([count - count % HEAD_SIZE, count % HEAD_SIZE], axis=1)
    marks = jnp.pad(marks.astype(jnp.bfloat16), ((0, 0), (0, HEAD_SIZE - 2)))

    half = HEAD_SIZE // 2
    freq = 10000.0 ** (-(jnp.arange(half, dtype=jnp.float32) * 2.0 / HEAD_SIZE))
    where = (positions[:, None] + step[None, :]).reshape(rows)
    angle = where[:, None].astype(jnp.float32) * freq
    cosine, sine = jnp.cos(angle), jnp.sin(angle)
    cosine = jnp.concatenate([cosine, cosine], axis=1)
    sine = jnp.concatenate([-sine, sine], axis=1)

    key_rows = rotated_prefix_keys[0]
    value_rows = shared_prefix_values[0]
    results, backs, own = [], [], []
    asked_first = far = None
    for i, (first, heads) in enumerate(zip(firsts, chunks, strict=True)):
        if staged:
            products = project(
                index, weights, mine, other, [settle(weights[6:], SETTLE)] if i == 0 and SETTLE else []
            )
            if i + 1 < len(chunks):
                started = first_round(weight_columns(i + 1), owners, weights[3:5])
                weights = second_round(started, owners)
            if i > 0 and TINY1:
                products = [products[0]] + [behind(p, before) for p in products[1:3]] + [products[3]]
            parts = line_sums(products, owners, inner, RS[min(i, 1)])
            if i + 1 < len(chunks):
                parts = after(parts, *weights)
        else:
            piece = qkv_weight[:, first * unit : (first + heads) * unit]
            parts = project_any(tokens, piece, owners, inner)
        if far is not None:
            if FARGATE:
                parts, far = lax.optimization_barrier((parts, far))
            backs.append(exchange(far.reshape(owners, capacity * DECODE_STEPS, -1)))
        packed, query, own_key, own_value = pack(
            parts, cosine, sine, route, marks, heads, int(first == 0)
        )
        own.append(near_part(query, own_key, own_value))
        before = passed_on(packed)
        if staged and PGATE:
            packed, weights = lax.optimization_barrier((packed, weights))
        width = packed.shape[1]
        asked = exchange(packed.reshape(owners, capacity * DECODE_STEPS, width))
        asked = asked.reshape(slots * DECODE_STEPS, width)
        asked_first = asked if first == 0 else asked_first
        far = prefix_part(asked, asked_first, key_rows, value_rows, first, heads)
    backs.append(exchange(far.reshape(owners, capacity * DECODE_STEPS, -1)))
    for back, kept in zip(backs, own, strict=True):
        results.append(join(back.reshape(slots * DECODE_STEPS, -1), route, *kept))
    return jnp.concatenate(results, axis=1).reshape(rows_dev, DECODE_STEPS, -1)


def solution(mesh):
    return jax.shard_map(
        on_device,
        mesh=mesh,
        in_specs=(
            P("wide", None, "narrow"),
            P("wide", "narrow"),
            P("wide", None, "narrow"),
            P("wide", None, "narrow"),
            P("wide", None),
            P("wide"),
        ),
        out_specs=P("wide", None, "narrow"),
        check_vma=False,
    )
```

time: 236 us -> 188 us (0.80)
  waiting for transfers between devices: 97.6 us -> 48.3 us
  local copies, waits for them, and re-layouts: 41.5 us -> 8.27 us
  blocking collectives: 0 us -> 20.1 us
  Pallas kernels: 25.9 us -> 39.2 us
  matrix products: 11.4 us -> 0 us
  starting transfers between devices: 56.1 us -> 64.1 us
  other arithmetic: 1.97 us -> 5.21 us
    all_to_all x3 -> x0, waiting for transfers between devices: 39.2 us -> none  [the longest x2 39.2 us: line_sums(): lax.all_to_all(partial.reshape(planes, rows, -1), 'wide', split_axis=0, c...]
    ppermute x1 -> x16, starting transfers between devices: 0.52 us -> 36.7 us  [the longest x8 30.1 us: along(): return lax.ppermute(block, 'wide', pairs)]
    all_to_all x0 -> x1, blocking collectives: none -> 20.1 us  [exchange(): lax.all_to_all(block, 'wide', split_axis=0, concat_axis=0, tiled=True)]
    ppermute x1 -> x16, waiting for transfers between devices: 0.01 us -> 20 us  [the longest x3 12.1 us: line_tokens(): blocks.append(lax.ppermute(block, ('wide', 'narrow'), pairs))]
    unnamed x39 -> x22, local copies, waits for them, and re-layouts: 22.3 us -> 3.38 us
    all_to_all x5 -> x3, waiting for transfers between devices: 24.8 us -> 8.62 us  [exchange(): lax.all_to_all(block, 'wide', split_axis=0, concat_axis=0, tiled=True)]
    all_to_all x3 -> x0, starting transfers between devices: 14.4 us -> none  [the longest x2 9.51 us: line_sums(): lax.all_to_all(partial.reshape(planes, rows, -1), 'wide', split_axis=0, c...]
    ppermute x12, waiting for transfers between devices: 33.6 us -> 19.7 us  [across(): return lax.ppermute(block, 'wide', [(i, i ^ mask) for i in range(owners)])]
  transfers between devices with their start and end apart: 21 -> 31, of which waited for: 11 -> 13; matrix products, arithmetic and copies ran while one was open for 19% -> 4% of each run, Pallas kernels for 10% -> 20%
where the time goes in v2:
time: 188 us; the launch traced here: 187 us
  starting transfers between devices  64.1 us (34%)
  waiting for transfers between devices  48.3 us (26%)
  Pallas kernels  39.2 us (21%)
  blocking collectives  20.1 us (11%)
  local copies, waits for them, and re-layouts  8.27 us (4%)
  other arithmetic  5.21 us (3%)
    ppermute x8, starting transfers between devices, along(): return lax.ppermute(block, 'wide', pairs)  30.1 us
    all_to_all x1, blocking collectives, exchange(): lax.all_to_all(block, 'wide', split_axis=0, concat_axis=0, tiled=True)  20.1 us
    ppermute x12, waiting for transfers between devices, across(): return lax.ppermute(block, 'wide', [(i, i ^ mask) for i in range(owners)])  19.7 us
    pallas_call x2, Pallas kernels, prefix_part(): pl.pallas_call(functools.partial(prefix_kernel, min(length, 512), heads),...  18.2 us
    all_to_all x3, starting transfers between devices, exchange(): lax.all_to_all(block, 'wide', split_axis=0, concat_axis=0, tiled=True)  14.3 us
    ppermute x12, starting transfers between devices, across(): return lax.ppermute(block, 'wide', [(i, i ^ mask) for i in range(owners)])  13.1 us
    ppermute x3, waiting for transfers between devices, line_tokens(): blocks.append(lax.ppermute(block, ('wide', 'narrow'), pairs))  12.1 us
    pallas_call x2, Pallas kernels, project(): pl.pallas_call(project_kernel, out_shape=[jax.ShapeDtypeStruct((size, col...  11.4 us
  transfers between devices with their start and end apart: 31, of which 13 were waited for; matrix products, arithmetic and copies ran while one was open for 4% of the time, Pallas kernels for 20%

profile of v2, /device:TPU:0, one launch (start us, length us, event | category | flops | bytes accessed | tf_op | source)
XLA Modules:
  0.0 186.9 jit_solution(7505949521368374150)
XLA Ops:
  0.0 1.7 fusion.6
  1.7 3.0 %collective-permute-start.21 = (bf16[160,1536]{1,0:T(8,128)(2,1)S(1)}, bf16[160,1536]{1,0:T(8,128)(2,1)}, u32[]{:S(2)}, u32[]{:S(2)}) collective-permute-start(bf16[160,1536]{1,0:T(8,128)(2,1)S(1)} %get-tuple-element.86.refs_1_), channel_id=1, source_target_pairs={{0,4},{2,6},{4,0},{6,2},{8,12},{10,14},{12,8},{14,10},{16,20},{18,... | collective-permute-start | bytes 1474568 | tf_op jit(solution)/shard_map/ppermute | solution.py:336
  4.7 1.5 collective-permute-start
  6.2 0.7 slice.37
  10.7 0.8 broadcast_select_fusion.3
  11.4 3.5 %collective-permute-start.9 = (bf16[128,1280]{1,0:T(8,128)(2,1)}, bf16[128,1280]{1,0:T(8,128)(2,1)}, u32[]{:S(2)}, u32[]{:S(2)}) collective-permute-start(bf16[128,1280]{1,0:T(8,128)(2,1)} %get-tuple-element.89), channel_id=1, source_target_pairs={{0,8},{2,10},{4,12},{6,14},{8,0},{10,2},{12,4},{14,6},{17,25},{19,... | collective-permute-start | bytes 983048 | tf_op jit(solution)/shard_map/ppermute | solution.py:375
  15.0 1.3 collective-permute-start.10
  16.5 4.2 %collective-permute-done.9.refs_9_ = bf16[128,1280]{1,0:T(8,128)(2,1)} collective-permute-done((bf16[128,1280]{1,0:T(8,128)(2,1)}, bf16[128,1280]{1,0:T(8,128)(2,1)}, u32[]{:S(2)}, u32[]{:S(2)}) %collective-permute-start.9) | collective-permute-done | bytes 327712 | tf_op jit(solution)/shard_map/ppermute | solution.py:375
  21.2 6.8 %collective-permute-done.20.refs_2_ = bf16[160,1536]{1,0:T(8,128)(2,1)} collective-permute-done((bf16[160,1536]{1,0:T(8,128)(2,1)S(1)}, bf16[160,1536]{1,0:T(8,128)(2,1)}, u32[]{:S(2)}, u32[]{:S(2)}) %collective-permute-start.20) | collective-permute-done | bytes 491552 | tf_op jit(solution)/shard_map/ppermute | solution.py:336
  28.5 1.3 collective-permute-start.11
  29.8 1.7 collective-permute-start.23
  31.9 7.8 %collective-permute-done.11.refs_11_ = bf16[128,1280]{1,0:T(8,128)(2,1)} collective-permute-done((bf16[128,1280]{1,0:T(8,128)(2,1)}, bf16[128,1280]{1,0:T(8,128)(2,1)}, u32[]{:S(2)}, u32[]{:S(2)}) %collective-permute-start.11) | collective-permute-done | bytes 327712 | tf_op jit(solution)/shard_map/ppermute | solution.py:375
  40.2 3.5 %collective-permute-done.22.refs_0_.refs_6_ = bf16[160,1536]{1,0:T(8,128)(2,1)S(1)} collective-permute-done((bf16[160,1536]{1,0:T(8,128)(2,1)}, bf16[160,1536]{1,0:T(8,128)(2,1)S(1)}, u32[]{:S(2)}, u32[]{:S(2)}) %collective-permute-start.22) | collective-permute-done | bytes 491552 | tf_op jit(solution)/shard_map/ppermute | solution.py:336
  43.8 0.9 fusion.2
  44.8 1.1 collective-permute-start.2
  47.0 1.0 copy-done.1
  48.0 1.0 copy-done.3
  49.7 5.5 %project.3 = (bf16[128,1536]{1,0:T(8,128)(2,1)S(1)}, bf16[128,1536]{1,0:T(8,128)(2,1)}, bf16[128,1536]{1,0:T(8,128)(2,1)}, bf16[128,1536]{1,0:T(8,128)(2,1)S(1)}) custom-call(s32[3]{0:T(128)S(1)} %pad_add_fusion.index, bf16[160,1536]{1,0:T(8,128)(2,1)S(1)} %get-tuple-element.85.refs_0_, bf16[160,1536]{1,0:T(8,128)(2,1)S(1)} %get-tuple-element.86.refs_1_, ...), custom_call_target="tpu_custom_call" | custom-call | flops 2013265920 | bytes 3932160 | tf_op jit(solution)/shard_map/project/pallas_call | solution.py:300
  55.3 2.4 %collective-permute-start.24 = (bf16[128,1536]{1,0:T(8,128)(2,1)}, bf16[128,1536]{1,0:T(8,128)(2,1)S(1)}, u32[]{:S(2)}, u32[]{:S(2)}) collective-permute-start(bf16[128,1536]{1,0:T(8,128)(2,1)} %get-tuple-element.54), channel_id=1, source_target_pairs={{0,8},{2,10},{4,12},{6,14},{8,0},{10,2},{12,4},{14,6},{16,24},{18,... | collective-permute-start | bytes 1179656 | tf_op jit(solution)/shard_map/ppermute | solution.py:390
  58.4 1.0 pad_maximum_fusion.1
  59.6 0.8 collective-permute-start.3
  60.9 1.5 collective-permute-start.6
  62.5 4.2 %collective-permute-done.24 = bf16[128,1536]{1,0:T(8,128)(2,1)S(1)} collective-permute-done((bf16[128,1536]{1,0:T(8,128)(2,1)}, bf16[128,1536]{1,0:T(8,128)(2,1)S(1)}, u32[]{:S(2)}, u32[]{:S(2)}) %collective-permute-start.24) | collective-permute-done | bytes 393248 | tf_op jit(solution)/shard_map/ppermute | solution.py:390
  66.7 1.1 collective-permute-start.7
  68.0 2.3 %collective-permute-start.27 = (bf16[128,1536]{1,0:T(8,128)(2,1)S(1)}, bf16[128,1536]{1,0:T(8,128)(2,1)S(1)}, u32[]{:S(2)}, u32[]{:S(2)}) collective-permute-start(bf16[128,1536]{1,0:T(8,128)(2,1)S(1)} %add_convert_fusion), channel_id=1, source_target_pairs={{0,16},{2,18},{4,20},{6,22},{16,0},{18,2},{20,4},{22,6},{8,24},{10... | collective-permute-start | bytes 1179656 | tf_op jit(solution)/shard_map/ppermute | solution.py:390
  70.4 3.5 %collective-permute-done.3.refs_3_ = bf16[160,1536]{1,0:T(8,128)(2,1)} collective-permute-done((bf16[160,1536]{1,0:T(8,128)(2,1)S(1)}, bf16[160,1536]{1,0:T(8,128)(2,1)}, u32[]{:S(2)}, u32[]{:S(2)}) %collective-permute-start.3) | collective-permute-done | bytes 491552 | tf_op jit(solution)/shard_map/ppermute | solution.py:336
  73.9 3.7 %collective-permute-start.26 = (bf16[128,1536]{1,0:T(8,128)(2,1)}, bf16[128,1536]{1,0:T(8,128)(2,1)S(1)}, u32[]{:S(2)}, u32[]{:S(2)}) collective-permute-start(bf16[128,1536]{1,0:T(8,128)(2,1)} %get-tuple-element.57), channel_id=1, source_target_pairs={{0,8},{2,10},{4,12},{6,14},{24,16},{26,18},{28,20},{30,22},{1,9},{... | collective-permute-start | bytes 1179656 | tf_op jit(solution)/shard_map/ppermute | solution.py:390
  77.7 5.8 %collective-permute-done.6.refs_6_ = bf16[160,1536]{1,0:T(8,128)(2,1)} collective-permute-done((bf16[160,1536]{1,0:T(8,128)(2,1)}, bf16[160,1536]{1,0:T(8,128)(2,1)}, u32[]{:S(2)}, u32[]{:S(2)}) %collective-permute-start.6) | collective-permute-done | bytes 491552 | tf_op jit(solution)/shard_map/ppermute | solution.py:336
  83.4 5.9 %project.2 = (bf16[128,1536]{1,0:T(8,128)(2,1)S(1)}, bf16[128,1536]{1,0:T(8,128)(2,1)}, bf16[128,1536]{1,0:T(8,128)(2,1)}, bf16[128,1536]{1,0:T(8,128)(2,1)S(1)}) custom-call(s32[3]{0:T(128)S(1)} %pad_add_fusion.index, bf16[160,1536]{1,0:T(8,128)(2,1)S(1)} %get-tuple-element.44.refs_0_, bf16[160,1536]{1,0:T(8,128)(2,1)S(1)} %get-tuple-element.45.refs_1_, ...), custom_call_target="tpu_custom_call" | custom-call | flops 2013265920 | bytes 3932160 | tf_op jit(solution)/shard_map/project/pallas_call | solution.py:300
  89.3 1.6 collective-permute-start.16
  91.7 1.4 pack.2
  93.1 5.5 %all-to-all-start = ((bf16[16,16,1152]{2,1,0:T(8,128)(2,1)}), bf16[16,16,1152]{2,1,0:T(8,128)(2,1)}, u32[]{:S(2)}, u32[]{:S(2)}) async-start(bf16[16,16,1152]{2,1,0:T(8,128)(2,1)} %bitcast.7), calls=%async_computation | async-start | bytes 1179648 | tf_op jit(solution)/shard_map/all_to_all | solution.py:433
  99.7 17.2 %collective-permute-start.19 = (bf16[128,1536]{1,0:T(8,128)(2,1)S(1)}, bf16[128,1536]{1,0:T(8,128)(2,1)S(1)}, u32[]{:S(2)}, u32[]{:S(2)}) collective-permute-start(bf16[128,1536]{1,0:T(8,128)(2,1)S(1)} %add_convert_fusion.1), channel_id=1, source_target_pairs={{0,16},{2,18},{4,20},{6,22},{16,0},{18,2},{20,4},{22,6},{8,24},{10... | collective-permute-start | bytes 1179656 | tf_op jit(solution)/shard_map/ppermute | solution.py:390
  116.9 1.5 collective-permute-start.18
  118.4 1.0 broadcast_select_fusion.2.refs_1_
  119.4 9.1 %prefix_part.2 = bf16[256,1152]{1,0:T(8,128)(2,1)} custom-call(bf16[256,1152]{1,0:T(8,128)(2,1)} %bitcast.8.asked.marks, bf16[256,1152]{1,0:T(8,128)(2,1)} %bitcast.8.asked.marks, bf16[2048,512]{1,0:T(8,128)(2,1)} %bitcast.31, bf16[2048,512]{1,0:T(8,128)(2,1)} %bitcast.33), custom_call_target="tpu_custom_call" | custom-call | flops 2147483648 | bytes 2097152 | tf_op jit(solution)/shard_map/prefix_part/pallas_call | solution.py:93
  128.6 2.9 %collective-permute-done.19.refs_4_ = bf16[128,1536]{1,0:T(8,128)(2,1)S(1)} collective-permute-done((bf16[128,1536]{1,0:T(8,128)(2,1)S(1)}, bf16[128,1536]{1,0:T(8,128)(2,1)S(1)}, u32[]{:S(2)}, u32[]{:S(2)}) %collective-permute-start.19) | collective-permute-done | bytes 393248 | tf_op jit(solution)/shard_map/ppermute | solution.py:390
  132.0 20.1 %all_to_all.20 = bf16[16,16,1024]{2,1,0:T(8,128)(2,1)} all-to-all(bf16[16,16,1024]{2,1,0:T(8,128)(2,1)S(1)} %bitcast.25), channel_id=1, replica_groups=mesh['wide'=16,'narrow'=2] {'wide'}, dimensions={0} | all-to-all | bytes 1048576 | tf_op jit(solution)/shard_map/all_to_all | solution.py:433
  152.1 4.0 %all-to-all-start.1 = ((bf16[16,16,1152]{2,1,0:T(8,128)(2,1)}), bf16[16,16,1152]{2,1,0:T(8,128)(2,1)S(1)}, u32[]{:S(2)}, u32[]{:S(2)}) async-start(bf16[16,16,1152]{2,1,0:T(8,128)(2,1)} %bitcast.26), calls=%async_computation.1 | async-start | bytes 1179648 | tf_op jit(solution)/shard_map/all_to_all | solution.py:433
  156.2 9.1 %prefix_part.3 = bf16[256,1152]{1,0:T(8,128)(2,1)} custom-call(bf16[256,1024]{1,0:T(8,128)(2,1)} %bitcast.28, bf16[256,1152]{1,0:T(8,128)(2,1)} %bitcast.8.asked.marks, bf16[2048,512]{1,0:T(8,128)(2,1)} %bitcast.32, bf16[2048,512]{1,0:T(8,128)(2,1)} %bitcast.34), custom_call_target="tpu_custom_call" | custom-call | flops 2147483648 | bytes 2097152 | tf_op jit(solution)/shard_map/prefix_part/pallas_call | solution.py:93
  165.3 2.7 %all-to-all-done.1 = bf16[16,16,1152]{2,1,0:T(8,128)(2,1)S(1)} async-done(((bf16[16,16,1152]{2,1,0:T(8,128)(2,1)}), bf16[16,16,1152]{2,1,0:T(8,128)(2,1)S(1)}, u32[]{:S(2)}, u32[]{:S(2)}) %all-to-all-start.1) | async-done | bytes 589856 | tf_op jit(solution)/shard_map/all_to_all | solution.py:433
  168.0 4.8 %all-to-all-start.3 = ((bf16[16,16,1152]{2,1,0:T(8,128)(2,1)}), bf16[16,16,1152]{2,1,0:T(8,128)(2,1)S(1)}, u32[]{:S(2)}, u32[]{:S(2)}) async-start(bf16[16,16,1152]{2,1,0:T(8,128)(2,1)} %bitcast.27), calls=%async_computation.3 | async-start | bytes 1179648 | tf_op jit(solution)/shard_map/all_to_all | solution.py:433
  172.8 2.0 %near_part.2 = (f32[128,1024]{1,0:T(8,128)S(1)}, f32[128,128]{1,0:T(8,128)S(1)}) custom-call(bf16[128,1024]{1,0:T(8,128)(2,1)S(1)} %get-tuple-element.67.query, bf16[128,256]{1,0:T(8,128)(2,1)S(1)} %get-tuple-element.68.key, bf16[128,256]{1,0:T(8,128)(2,1)S(1)} %get-tuple-element.69.value), custom_call_target="tpu_custom_call" | custom-call | flops 67108864 | bytes 1048576 | tf_op jit(solution)/shard_map/near_part/pallas_call | solution.py:190
  174.8 2.0 %near_part.3 = (f32[128,1024]{1,0:T(8,128)S(1)}, f32[128,128]{1,0:T(8,128)S(1)}) custom-call(bf16[128,1024]{1,0:T(8,128)(2,1)S(1)} %get-tuple-element.78.query, bf16[128,256]{1,0:T(8,128)(2,1)S(1)} %get-tuple-element.79.key, bf16[128,256]{1,0:T(8,128)(2,1)S(1)} %get-tuple-element.80.value), custom_call_target="tpu_custom_call" | custom-call | flops 67108864 | bytes 1048576 | tf_op jit(solution)/shard_map/near_part/pallas_call | solution.py:190
  176.8 1.5 join.2
  178.3 5.9 %all-to-all-done.3 = bf16[16,16,1152]{2,1,0:T(8,128)(2,1)S(1)} async-done(((bf16[16,16,1152]{2,1,0:T(8,128)(2,1)}), bf16[16,16,1152]{2,1,0:T(8,128)(2,1)S(1)}, u32[]{:S(2)}, u32[]{:S(2)}) %all-to-all-start.3) | async-done | bytes 589856 | tf_op jit(solution)/shard_map/all_to_all | solution.py:433
  184.2 1.5 join.3
  185.7 1.1 reshape.150
  (80 shorter events, 10.6 us)
Async XLA Ops:
  0.0 7.4 %copy-start.9 = (s32[64,1]{0,1:T(1,128)S(1)}, s32[64,1]{0,1:T(1,128)}, u32[]{:S(2)}) copy-start(s32[64,1]{0,1:T(1,128)} %param.10) | copy-start | bytes 772
  0.0 9.9 %copy-start.8 = (bf16[64,2,2560]{2,1,0:T(2,128)(2,1)S(1)}, bf16[64,2,2560]{2,1,0:T(2,128)(2,1)}, u32[]{:S(2)}) copy-start(bf16[64,2,2560]{2,1,0:T(2,128)(2,1)} %param.6) | copy-start | bytes 1966084
  1.7 13.2 %copy-start.10 = (s32[64]{0:T(128)S(1)}, s32[64]{0:T(128)}, u32[]{:S(2)}) copy-start(s32[64]{0:T(128)} %param.11) | copy-start | bytes 772
  1.7 28.1 %collective-permute-start.21 = (bf16[160,1536]{1,0:T(8,128)(2,1)S(1)}, bf16[160,1536]{1,0:T(8,128)(2,1)}, u32[]{:S(2)}, u32[]{:S(2)}) collective-permute-start(bf16[160,1536]{1,0:T(8,128)(2,1)S(1)} %get-tuple-element.86.refs_1_), channel_id=1, source_target_pairs={{0,4},{2,6},{4,0},{6,2},{8,12},{10,14},{12,8},{14,10},{16,20},{18,... | collective-permute-start | bytes 1474568 | tf_op jit(solution)/shard_map/ppermute | solution.py:336
  4.7 34.9 %collective-permute-start = (bf16[160,1536]{1,0:T(8,128)(2,1)S(1)}, bf16[160,1536]{1,0:T(8,128)(2,1)}, u32[]{:S(2)}, u32[]{:S(2)}) collective-permute-start(bf16[160,1536]{1,0:T(8,128)(2,1)S(1)} %get-tuple-element.86.refs_1_), channel_id=1, source_target_pairs={{0,2},{2,0},{4,6},{6,4},{8,10},{10,8},{12,14},{14,12},{16,18},{18,... | collective-permute-start | bytes 1474568 | tf_op jit(solution)/shard_map/ppermute | solution.py:336
  6.9 1.2 collective-permute-start.8
  6.9 21.1 %collective-permute-start.20 = (bf16[160,1536]{1,0:T(8,128)(2,1)S(1)}, bf16[160,1536]{1,0:T(8,128)(2,1)}, u32[]{:S(2)}, u32[]{:S(2)}) collective-permute-start(bf16[160,1536]{1,0:T(8,128)(2,1)S(1)} %get-tuple-element.85.refs_0_), channel_id=1, source_target_pairs={{0,2},{2,0},{4,6},{6,4},{8,10},{10,8},{12,14},{14,12},{16,18},{18,... | collective-permute-start | bytes 1474568 | tf_op jit(solution)/shard_map/ppermute | solution.py:336
  11.4 9.3 %collective-permute-start.9 = (bf16[128,1280]{1,0:T(8,128)(2,1)}, bf16[128,1280]{1,0:T(8,128)(2,1)}, u32[]{:S(2)}, u32[]{:S(2)}) collective-permute-start(bf16[128,1280]{1,0:T(8,128)(2,1)} %get-tuple-element.89), channel_id=1, source_target_pairs={{0,8},{2,10},{4,12},{6,14},{8,0},{10,2},{12,4},{14,6},{17,25},{19,... | collective-permute-start | bytes 983048 | tf_op jit(solution)/shard_map/ppermute | solution.py:375
  15.0 13.5 %collective-permute-start.10 = (bf16[128,1280]{1,0:T(8,128)(2,1)S(1)}, bf16[128,1280]{1,0:T(8,128)(2,1)}, u32[]{:S(2)}, u32[]{:S(2)}) collective-permute-start(bf16[128,1280]{1,0:T(8,128)(2,1)S(1)} %get-tuple-element.90.refs_8_), channel_id=1, source_target_pairs={{1,17},{3,19},{5,21},{7,23},{9,25},{11,27},{13,29},{15,31},{16,0},... | collective-permute-start | bytes 983048 | tf_op jit(solution)/shard_map/ppermute | solution.py:375
  20.7 19.4 %collective-permute-start.1 = (bf16[160,1536]{1,0:T(8,128)(2,1)S(1)}, bf16[160,1536]{1,0:T(8,128)(2,1)}, u32[]{:S(2)}, u32[]{:S(2)}) collective-permute-start(bf16[160,1536]{1,0:T(8,128)(2,1)S(1)} %get-tuple-element.85.refs_0_), channel_id=1, source_target_pairs={{0,4},{2,6},{4,0},{6,2},{8,12},{10,14},{12,8},{14,10},{16,20},{18,... | collective-permute-start | bytes 1474568 | tf_op jit(solution)/shard_map/ppermute | solution.py:336
  28.0 15.7 %collective-permute-start.22 = (bf16[160,1536]{1,0:T(8,128)(2,1)}, bf16[160,1536]{1,0:T(8,128)(2,1)S(1)}, u32[]{:S(2)}, u32[]{:S(2)}) collective-permute-start(bf16[160,1536]{1,0:T(8,128)(2,1)} %collective-permute-done.20.refs_2_), channel_id=1, source_target_pairs={{0,4},{2,6},{4,0},{6,2},{8,12},{10,14},{12,8},{14,10},{16,20},{18,... | collective-permute-start | bytes 1474568 | tf_op jit(solution)/shard_map/ppermute | solution.py:336
  28.5 11.2 %collective-permute-start.11 = (bf16[128,1280]{1,0:T(8,128)(2,1)}, bf16[128,1280]{1,0:T(8,128)(2,1)}, u32[]{:S(2)}, u32[]{:S(2)}) collective-permute-start(bf16[128,1280]{1,0:T(8,128)(2,1)} %get-tuple-element.89), channel_id=1, source_target_pairs={{1,25},{3,27},{5,29},{7,31},{9,17},{11,19},{13,21},{15,23},{16,8},... | collective-permute-start | bytes 983048 | tf_op jit(solution)/shard_map/ppermute | solution.py:375
  29.8 15.0 %collective-permute-start.23 = (bf16[160,1536]{1,0:T(8,128)(2,1)}, bf16[160,1536]{1,0:T(8,128)(2,1)S(1)}, u32[]{:S(2)}, u32[]{:S(2)}) collective-permute-start(bf16[160,1536]{1,0:T(8,128)(2,1)} %collective-permute-done.21.refs_5_), channel_id=1, source_target_pairs={{0,2},{2,0},{4,6},{6,4},{8,10},{10,8},{12,14},{14,12},{16,18},{18,... | collective-permute-start | bytes 1474568 | tf_op jit(solution)/shard_map/ppermute | solution.py:336
  39.6 6.8 %collective-permute-start.12 = (bf16[128,1280]{1,0:T(8,128)(2,1)S(1)}, bf16[128,1280]{1,0:T(8,128)(2,1)}, u32[]{:S(2)}, u32[]{:S(2)}) collective-permute-start(bf16[128,1280]{1,0:T(8,128)(2,1)S(1)} %get-tuple-element.90.refs_8_), channel_id=1, source_target_pairs={{0,1},{1,0},{2,3},{3,2},{4,5},{5,4},{6,7},{7,6},{8,9},{9,8},{10,11... | collective-permute-start | bytes 983048 | tf_op jit(solution)/shard_map/ppermute | solution.py:380
  39.6 7.3 %collective-permute-start.13 = (bf16[128,1280]{1,0:T(8,128)(2,1)}, bf16[128,1280]{1,0:T(8,128)(2,1)}, u32[]{:S(2)}, u32[]{:S(2)}) collective-permute-start(bf16[128,1280]{1,0:T(8,128)(2,1)} %collective-permute-done.9.refs_9_), channel_id=1, source_target_pairs={{0,1},{1,0},{2,3},{3,2},{4,5},{5,4},{6,7},{7,6},{8,9},{9,8},{10,11... | collective-permute-start | bytes 983048 | tf_op jit(solution)/shard_map/ppermute | solution.py:380
  40.2 6.8 %collective-permute-start.14 = (bf16[128,1280]{1,0:T(8,128)(2,1)}, bf16[128,1280]{1,0:T(8,128)(2,1)}, u32[]{:S(2)}, u32[]{:S(2)}) collective-permute-start(bf16[128,1280]{1,0:T(8,128)(2,1)} %collective-permute-done.10.refs_10_), channel_id=1, source_target_pairs={{0,1},{1,0},{2,3},{3,2},{4,5},{5,4},{6,7},{7,6},{8,9},{9,8},{10,11... | collective-permute-start | bytes 983048 | tf_op jit(solution)/shard_map/ppermute | solution.py:380
  43.7 2.1 %copy-start = (bf16[160,1536]{1,0:T(8,128)(2,1)}, bf16[160,1536]{1,0:T(8,128)(2,1)S(1)}, u32[]{:S(2)}) copy-start(bf16[160,1536]{1,0:T(8,128)(2,1)S(1)} %collective-permute-done.22.refs_0_.refs_6_) | copy-start | bytes 1474564
  43.8 3.2 %collective-permute-start.15 = (bf16[128,1280]{1,0:T(8,128)(2,1)}, bf16[128,1280]{1,0:T(8,128)(2,1)}, u32[]{:S(2)}, u32[]{:S(2)}) collective-permute-start(bf16[128,1280]{1,0:T(8,128)(2,1)} %collective-permute-done.11.refs_11_), channel_id=1, source_target_pairs={{0,1},{1,0},{2,3},{3,2},{4,5},{5,4},{6,7},{7,6},{8,9},{9,8},{10,11... | collective-permute-start | bytes 983048 | tf_op jit(solution)/shard_map/ppermute | solution.py:380
  44.8 1.1 copy-start.2
  44.8 15.7 %collective-permute-start.2 = (bf16[160,1536]{1,0:T(8,128)(2,1)S(1)}, bf16[160,1536]{1,0:T(8,128)(2,1)}, u32[]{:S(2)}, u32[]{:S(2)}) collective-permute-start(bf16[160,1536]{1,0:T(8,128)(2,1)S(1)} %get-tuple-element.44.refs_0_), channel_id=1, source_target_pairs={{0,2},{2,0},{4,6},{6,4},{8,10},{10,8},{12,14},{14,12},{16,18},{18,... | collective-permute-start | bytes 1474568 | tf_op jit(solution)/shard_map/ppermute | solution.py:336
  46.5 14.5 %collective-permute-start.5 = (bf16[160,1536]{1,0:T(8,128)(2,1)S(1)}, bf16[160,1536]{1,0:T(8,128)(2,1)}, u32[]{:S(2)}, u32[]{:S(2)}) collective-permute-start(bf16[160,1536]{1,0:T(8,128)(2,1)S(1)} %get-tuple-element.45.refs_1_), channel_id=1, source_target_pairs={{0,4},{2,6},{4,0},{6,2},{8,12},{10,14},{12,8},{14,10},{16,20},{18,... | collective-permute-start | bytes 1474568 | tf_op jit(solution)/shard_map/ppermute | solution.py:336
  47.0 1.0 copy-start.1
  48.0 1.0 copy-start.3
  49.1 0.7 copy-start.4
  55.3 11.4 %collective-permute-start.24 = (bf16[128,1536]{1,0:T(8,128)(2,1)}, bf16[128,1536]{1,0:T(8,128)(2,1)S(1)}, u32[]{:S(2)}, u32[]{:S(2)}) collective-permute-start(bf16[128,1536]{1,0:T(8,128)(2,1)} %get-tuple-element.54), channel_id=1, source_target_pairs={{0,8},{2,10},{4,12},{6,14},{8,0},{10,2},{12,4},{14,6},{16,24},{18,... | collective-permute-start | bytes 1179656 | tf_op jit(solution)/shard_map/ppermute | solution.py:390
  57.7 10.2 %collective-permute-start.25 = (bf16[128,1536]{1,0:T(8,128)(2,1)}, bf16[128,1536]{1,0:T(8,128)(2,1)S(1)}, u32[]{:S(2)}, u32[]{:S(2)}) collective-permute-start(bf16[128,1536]{1,0:T(8,128)(2,1)} %get-tuple-element.57), channel_id=1, source_target_pairs={{8,16},{10,18},{12,20},{14,22},{16,8},{18,10},{20,12},{22,14},{9,1... | collective-permute-start | bytes 1179656 | tf_op jit(solution)/shard_map/ppermute | solution.py:390
  59.6 14.3 %collective-permute-start.3 = (bf16[160,1536]{1,0:T(8,128)(2,1)S(1)}, bf16[160,1536]{1,0:T(8,128)(2,1)}, u32[]{:S(2)}, u32[]{:S(2)}) collective-permute-start(bf16[160,1536]{1,0:T(8,128)(2,1)S(1)} %get-tuple-element.45.refs_1_), channel_id=1, source_target_pairs={{0,2},{2,0},{4,6},{6,4},{8,10},{10,8},{12,14},{14,12},{16,18},{18,... | collective-permute-start | bytes 1474568 | tf_op jit(solution)/shard_map/ppermute | solution.py:336
  60.4 17.2 %collective-permute-start.4 = (bf16[160,1536]{1,0:T(8,128)(2,1)S(1)}, bf16[160,1536]{1,0:T(8,128)(2,1)}, u32[]{:S(2)}, u32[]{:S(2)}) collective-permute-start(bf16[160,1536]{1,0:T(8,128)(2,1)S(1)} %get-tuple-element.44.refs_0_), channel_id=1, source_target_pairs={{0,4},{2,6},{4,0},{6,2},{8,12},{10,14},{12,8},{14,10},{16,20},{18,... | collective-permute-start | bytes 1474568 | tf_op jit(solution)/shard_map/ppermute | solution.py:336
  60.9 22.5 %collective-permute-start.6 = (bf16[160,1536]{1,0:T(8,128)(2,1)}, bf16[160,1536]{1,0:T(8,128)(2,1)}, u32[]{:S(2)}, u32[]{:S(2)}) collective-permute-start(bf16[160,1536]{1,0:T(8,128)(2,1)} %collective-permute-done.2.refs_2_), channel_id=1, source_target_pairs={{0,4},{2,6},{4,0},{6,2},{8,12},{10,14},{12,8},{14,10},{16,20},{18,... | collective-permute-start | bytes 1474568 | tf_op jit(solution)/shard_map/ppermute | solution.py:336
  66.7 16.7 %copy-start.5 = (bf16[128,1536]{1,0:T(8,128)(2,1)}, bf16[128,1536]{1,0:T(8,128)(2,1)S(1)}, u32[]{:S(2)}) copy-start(bf16[128,1536]{1,0:T(8,128)(2,1)S(1)} %collective-permute-done.24) | copy-start | bytes 1179652
  66.7 16.7 %collective-permute-start.7 = (bf16[160,1536]{1,0:T(8,128)(2,1)}, bf16[160,1536]{1,0:T(8,128)(2,1)}, u32[]{:S(2)}, u32[]{:S(2)}) collective-permute-start(bf16[160,1536]{1,0:T(8,128)(2,1)} %collective-permute-done.5.refs_5_), channel_id=1, source_target_pairs={{0,2},{2,0},{4,6},{6,4},{8,10},{10,8},{12,14},{14,12},{16,18},{18,... | collective-permute-start | bytes 1474568 | tf_op jit(solution)/shard_map/ppermute | solution.py:336
  68.0 23.6 %collective-permute-start.27 = (bf16[128,1536]{1,0:T(8,128)(2,1)S(1)}, bf16[128,1536]{1,0:T(8,128)(2,1)S(1)}, u32[]{:S(2)}, u32[]{:S(2)}) collective-permute-start(bf16[128,1536]{1,0:T(8,128)(2,1)S(1)} %add_convert_fusion), channel_id=1, source_target_pairs={{0,16},{2,18},{4,20},{6,22},{16,0},{18,2},{20,4},{22,6},{8,24},{10... | collective-permute-start | bytes 1179656 | tf_op jit(solution)/shard_map/ppermute | solution.py:390
  73.9 17.8 %collective-permute-start.26 = (bf16[128,1536]{1,0:T(8,128)(2,1)}, bf16[128,1536]{1,0:T(8,128)(2,1)S(1)}, u32[]{:S(2)}, u32[]{:S(2)}) collective-permute-start(bf16[128,1536]{1,0:T(8,128)(2,1)} %get-tuple-element.57), channel_id=1, source_target_pairs={{0,8},{2,10},{4,12},{6,14},{24,16},{26,18},{28,20},{30,22},{1,9},{... | collective-permute-start | bytes 1179656 | tf_op jit(solution)/shard_map/ppermute | solution.py:390
  83.4 8.2 %copy-start.6 = (bf16[128,1536]{1,0:T(8,128)(2,1)S(1)}, bf16[128,1536]{1,0:T(8,128)(2,1)}, u32[]{:S(2)}) copy-start(bf16[128,1536]{1,0:T(8,128)(2,1)} %copy-done.5) | copy-start | bytes 1179652
  89.3 9.7 %collective-permute-start.16 = (bf16[128,1536]{1,0:T(8,128)(2,1)}, bf16[128,1536]{1,0:T(8,128)(2,1)S(1)}, u32[]{:S(2)}, u32[]{:S(2)}) collective-permute-start(bf16[128,1536]{1,0:T(8,128)(2,1)} %get-tuple-element.47), channel_id=1, source_target_pairs={{0,8},{2,10},{4,12},{6,14},{8,0},{10,2},{12,4},{14,6},{16,24},{18,... | collective-permute-start | bytes 1179656 | tf_op jit(solution)/shard_map/ppermute | solution.py:390
  91.0 8.0 %collective-permute-start.17 = (bf16[128,1536]{1,0:T(8,128)(2,1)}, bf16[128,1536]{1,0:T(8,128)(2,1)S(1)}, u32[]{:S(2)}, u32[]{:S(2)}) collective-permute-start(bf16[128,1536]{1,0:T(8,128)(2,1)} %get-tuple-element.50), channel_id=1, source_target_pairs={{8,16},{10,18},{12,20},{14,22},{16,8},{18,10},{20,12},{22,14},{9,1... | collective-permute-start | bytes 1179656 | tf_op jit(solution)/shard_map/ppermute | solution.py:390
  93.1 26.3 %all-to-all-start = ((bf16[16,16,1152]{2,1,0:T(8,128)(2,1)}), bf16[16,16,1152]{2,1,0:T(8,128)(2,1)}, u32[]{:S(2)}, u32[]{:S(2)}) async-start(bf16[16,16,1152]{2,1,0:T(8,128)(2,1)} %bitcast.7), calls=%async_computation | async-start | bytes 1179648 | tf_op jit(solution)/shard_map/all_to_all | solution.py:433
  99.0 0.7 copy-start.7
  99.7 31.7 %collective-permute-start.19 = (bf16[128,1536]{1,0:T(8,128)(2,1)S(1)}, bf16[128,1536]{1,0:T(8,128)(2,1)S(1)}, u32[]{:S(2)}, u32[]{:S(2)}) collective-permute-start(bf16[128,1536]{1,0:T(8,128)(2,1)S(1)} %add_convert_fusion.1), channel_id=1, source_target_pairs={{0,16},{2,18},{4,20},{6,22},{16,0},{18,2},{20,4},{22,6},{8,24},{10... | collective-permute-start | bytes 1179656 | tf_op jit(solution)/shard_map/ppermute | solution.py:390
  116.9 14.5 %collective-permute-start.18 = (bf16[128,1536]{1,0:T(8,128)(2,1)}, bf16[128,1536]{1,0:T(8,128)(2,1)S(1)}, u32[]{:S(2)}, u32[]{:S(2)}) collective-permute-start(bf16[128,1536]{1,0:T(8,128)(2,1)} %get-tuple-element.50), channel_id=1, source_target_pairs={{0,8},{2,10},{4,12},{6,14},{24,16},{26,18},{28,20},{30,22},{1,9},{... | collective-permute-start | bytes 1179656 | tf_op jit(solution)/shard_map/ppermute | solution.py:390
  152.1 15.9 %all-to-all-start.1 = ((bf16[16,16,1152]{2,1,0:T(8,128)(2,1)}), bf16[16,16,1152]{2,1,0:T(8,128)(2,1)S(1)}, u32[]{:S(2)}, u32[]{:S(2)}) async-start(bf16[16,16,1152]{2,1,0:T(8,128)(2,1)} %bitcast.26), calls=%async_computation.1 | async-start | bytes 1179648 | tf_op jit(solution)/shard_map/all_to_all | solution.py:433
  168.0 16.2 %all-to-all-start.3 = ((bf16[16,16,1152]{2,1,0:T(8,128)(2,1)}), bf16[16,16,1152]{2,1,0:T(8,128)(2,1)S(1)}, u32[]{:S(2)}, u32[]{:S(2)}) async-start(bf16[16,16,1152]{2,1,0:T(8,128)(2,1)} %bitcast.27), calls=%async_computation.3 | async-start | bytes 1179648 | tf_op jit(solution)/shard_map/all_to_all | solution.py:433

commit v3 on v2

--- a/solution.py
+++ b/solution.py
@@ -15,17 +15,7 @@
 SCALE = 1.0 / HEAD_SIZE**0.5
 LOG2E = 1.4426950408889634
 FLOOR = 512
-RS = ("relay2", "relay2")
-FARGATE = True
-P2GATE = False
-PROJ_MB = 40
-TINY0 = True
-TINY1 = False
-SETTLE = 20000000
-KP = 1.0
-KA = 1.0
-PGATE = False
-KVLATE = False
+SETTLE = 20_000_000
 CHUNKS = (2, 2)
 PIECES = 3
 NT = (((1,), (1,)), ((), ()))
@@ -91,7 +81,7 @@
     last = marks.shape[1] // HEAD_SIZE - 1
     block = pl.BlockSpec((length, HEAD_SIZE), lambda i: (0, first + i))
     return pl.pallas_call(
-        functools.partial(prefix_kernel, min(length, 512), heads),
+        functools.partial(prefix_kernel, min(length, 256), heads),
         grid=(heads,),
         out_shape=jax.ShapeDtypeStruct((rows, wide + HEAD_SIZE), jnp.bfloat16),
         in_specs=[
@@ -101,9 +91,9 @@
             block,
         ],
         out_specs=pl.BlockSpec((rows, wide + HEAD_SIZE), lambda i: (0, 0)),
-        compiler_params=pltpu.CompilerParams(vmem_limit_bytes=56 * 2**20),
+        compiler_params=pltpu.CompilerParams(vmem_limit_bytes=40 * 2**20),
         cost_estimate=pl.CostEstimate(
-            flops=int(KA * 4 * rows * length * wide),
+            flops=4 * rows * length * wide,
             bytes_accessed=4 * length * heads * HEAD_SIZE,
             transcendentals=rows * length * heads * GROUP,
         ),
@@ -308,9 +298,9 @@
             pltpu.VMEM((4 * size, depth), jnp.bfloat16),
             pltpu.VMEM((depth, columns), jnp.bfloat16),
         ],
-        compiler_params=pltpu.CompilerParams(vmem_limit_bytes=PROJ_MB * 2**20),
+        compiler_params=pltpu.CompilerParams(vmem_limit_bytes=40 * 2**20),
         cost_estimate=pl.CostEstimate(
-            flops=int(KP * 8 * size * depth * columns), bytes_accessed=2 * depth * columns, transcendentals=0
+            flops=8 * size * depth * columns, bytes_accessed=2 * depth * columns, transcendentals=0
         ),
         name="project",
     )(index, *pieces, *mine, *other, *marks)
@@ -345,7 +335,7 @@
 
 
 def second_round(blocks, owners):
-    upper, lower, upper_1, lower_2 = lax.optimization_barrier(blocks) if P2GATE else blocks
+    upper, lower, upper_1, lower_2 = blocks
     upper_2, lower_1 = across(upper, 2, owners), across(lower, 1, owners)
     upper_3, lower_3 = across(upper_1, 2, owners), across(lower_2, 1, owners)
     return [upper, lower, upper_1, lower_1, upper_2, lower_2, upper_3, lower_3]
@@ -380,7 +370,7 @@
     return [lax.ppermute(block, "narrow", [(0, 1), (1, 0)]) for block in blocks]
 
 
-def line_sums(partial, owners, inner, how):
+def line_sums(partial, owners, inner):
     own, first, second, third = partial
     plane = lax.axis_index("wide") // inner
     end = (plane == 0) | (plane == 3)
@@ -389,15 +379,9 @@
         pairs = [(a * inner + j, b * inner + j) for a, b in hops for j in range(inner)]
         return lax.ppermute(block, "wide", pairs)
 
-    if how == "direct":
-        near = along(first, [(0, 1), (1, 0), (2, 3), (3, 2)])
-        mid = along(second, [(0, 3), (3, 0), (1, 2), (2, 1)])
-        far = along(third, [(0, 2), (2, 0), (1, 3), (3, 1)])
-        return [own, near, mid, far]
     near = along(first, [(0, 1), (1, 0), (2, 3), (3, 2)])
     middle = along(second, [(1, 2), (2, 1)])
-    if how == "relay2":
-        near, middle, second = lax.optimization_barrier((near, middle, second))
+    near, middle, second = lax.optimization_barrier((near, middle, second))
     outer = along(second, [(0, 1), (3, 2)])
     passed = jnp.where(end, 0, near.astype(jnp.float32))
     third = (third.astype(jnp.float32) + passed).astype(jnp.bfloat16)
@@ -454,7 +438,7 @@
             return qkv_weight[:, firsts[i] * unit : (firsts[i] + chunks[i]) * unit]
 
         started = first_round(weight_columns(0), owners, None)
-        mine = line_tokens(tokens, owners, inner, passed_on(started[0]) if TINY0 else None)
+        mine = line_tokens(tokens, owners, inner, passed_on(started[0]))
         weights, other = second_round(started, owners), from_other_core(mine)
         index = jnp.stack(
             [
@@ -493,30 +477,24 @@
     for i, (first, heads) in enumerate(zip(firsts, chunks, strict=True)):
         if staged:
             products = project(
-                index, weights, mine, other, [settle(weights[6:], SETTLE)] if i == 0 and SETTLE else []
+                index, weights, mine, other, [settle(weights[6:], SETTLE)] if i == 0 else []
             )
             if i + 1 < len(chunks):
                 started = first_round(weight_columns(i + 1), owners, weights[3:5])
                 weights = second_round(started, owners)
-            if i > 0 and TINY1:
-                products = [products[0]] + [behind(p, before) for p in products[1:3]] + [products[3]]
-            parts = line_sums(products, owners, inner, RS[min(i, 1)])
+            parts = line_sums(products, owners, inner)
             if i + 1 < len(chunks):
                 parts = after(parts, *weights)
         else:
             piece = qkv_weight[:, first * unit : (first + heads) * unit]
             parts = project_any(tokens, piece, owners, inner)
         if far is not None:
-            if FARGATE:
-                parts, far = lax.optimization_barrier((parts, far))
+            parts, far = lax.optimization_barrier((parts, far))
             backs.append(exchange(far.reshape(owners, capacity * DECODE_STEPS, -1)))
         packed, query, own_key, own_value = pack(
             parts, cosine, sine, route, marks, heads, int(first == 0)
         )
         own.append(near_part(query, own_key, own_value))
-        before = passed_on(packed)
-        if staged and PGATE:
-            packed, weights = lax.optimization_barrier((packed, weights))
         width = packed.shape[1]
         asked = exchange(packed.reshape(owners, capacity * DECODE_STEPS, width))
         asked = asked.reshape(slots * DECODE_STEPS, width)

time: 188 us -> 186 us (0.989)
  local copies, waits for them, and re-layouts: 8.27 us -> 14.8 us
  waiting for transfers between devices: 48.3 us -> 43.4 us
  blocking collectives: 20.1 us -> 16.6 us
  Pallas kernels: 39.2 us -> 36.8 us
  starting transfers between devices: 64.1 us -> 66.1 us
    unnamed x22 -> x32, local copies, waits for them, and re-layouts: 3.38 us -> 9.12 us
    all_to_all x1, blocking collectives: 20.1 us -> 16.6 us  [exchange(): lax.all_to_all(block, 'wide', split_axis=0, concat_axis=0, tiled=True)]
    all_to_all x3, waiting for transfers between devices: 8.62 us -> 6.2 us  [exchange(): lax.all_to_all(block, 'wide', split_axis=0, concat_axis=0, tiled=True)]
    pallas_call x2, Pallas kernels: 18.2 us -> 15.9 us  [prefix_part(): pl.pallas_call(functools.partial(prefix_kernel, min(length, 256), heads),...]
  transfers between devices with their start and end apart: 31 -> 31, of which waited for: 13 -> 12; matrix products, arithmetic and copies ran while one was open for 4% -> 5% of each run, Pallas kernels for 20% -> 19%
where the time goes in v3:
time: 186 us; the launch traced here: 185 us
  starting transfers between devices  66.1 us (36%)
  waiting for transfers between devices  43.4 us (23%)
  Pallas kernels  36.8 us (20%)
  blocking collectives  16.6 us (9%)
  local copies, waits for them, and re-layouts  14.8 us (8%)
  other arithmetic  6 us (3%)
    ppermute x8, starting transfers between devices, along(): return lax.ppermute(block, 'wide', pairs)  30.6 us
    ppermute x12, waiting for transfers between devices, across(): return lax.ppermute(block, 'wide', [(i, i ^ mask) for i in range(owners)])  19.6 us
    all_to_all x1, blocking collectives, exchange(): lax.all_to_all(block, 'wide', split_axis=0, concat_axis=0, tiled=True)  16.6 us
    pallas_call x2, Pallas kernels, prefix_part(): pl.pallas_call(functools.partial(prefix_kernel, min(length, 256), heads),...  15.9 us
    all_to_all x3, starting transfers between devices, exchange(): lax.all_to_all(block, 'wide', split_axis=0, concat_axis=0, tiled=True)  15.7 us
    ppermute x12, starting transfers between devices, across(): return lax.ppermute(block, 'wide', [(i, i ^ mask) for i in range(owners)])  13.2 us
    ppermute x3, waiting for transfers between devices, line_tokens(): blocks.append(lax.ppermute(block, ('wide', 'narrow'), pairs))  11.5 us
    pallas_call x2, Pallas kernels, project(): pl.pallas_call(project_kernel, out_shape=[jax.ShapeDtypeStruct((size, col...  11.4 us
  transfers between devices with their start and end apart: 31, of which 12 were waited for; matrix products, arithmetic and copies ran while one was open for 5% of the time, Pallas kernels for 19%

profile of v3, /device:TPU:0, one launch (start us, length us, event | category | flops | bytes accessed | tf_op | source)
XLA Modules:
  0.0 185.4 jit_solution(13273702123720627976)
XLA Ops:
  0.0 1.7 fusion.6
  1.7 3.0 %collective-permute-start.21 = (bf16[160,1536]{1,0:T(8,128)(2,1)S(1)}, bf16[160,1536]{1,0:T(8,128)(2,1)}, u32[]{:S(2)}, u32[]{:S(2)}) collective-permute-start(bf16[160,1536]{1,0:T(8,128)(2,1)S(1)} %get-tuple-element.86.refs_1_), channel_id=1, source_target_pairs={{0,4},{2,6},{4,0},{6,2},{8,12},{10,14},{12,8},{14,10},{16,20},{18,... | collective-permute-start | bytes 1474568 | tf_op jit(solution)/shard_map/ppermute | solution.py:326
  4.7 1.5 collective-permute-start
  11.4 3.5 %collective-permute-start.9 = (bf16[128,1280]{1,0:T(8,128)(2,1)}, bf16[128,1280]{1,0:T(8,128)(2,1)}, u32[]{:S(2)}, u32[]{:S(2)}) collective-permute-start(bf16[128,1280]{1,0:T(8,128)(2,1)} %get-tuple-element.89), channel_id=1, source_target_pairs={{0,8},{2,10},{4,12},{6,14},{8,0},{10,2},{12,4},{14,6},{17,25},{19,... | collective-permute-start | bytes 983048 | tf_op jit(solution)/shard_map/ppermute | solution.py:365
  15.0 1.3 collective-permute-start.10
  16.5 4.2 %collective-permute-done.9.refs_9_ = bf16[128,1280]{1,0:T(8,128)(2,1)} collective-permute-done((bf16[128,1280]{1,0:T(8,128)(2,1)}, bf16[128,1280]{1,0:T(8,128)(2,1)}, u32[]{:S(2)}, u32[]{:S(2)}) %collective-permute-start.9) | collective-permute-done | bytes 327712 | tf_op jit(solution)/shard_map/ppermute | solution.py:365
  21.2 6.8 %collective-permute-done.20.refs_2_ = bf16[160,1536]{1,0:T(8,128)(2,1)} collective-permute-done((bf16[160,1536]{1,0:T(8,128)(2,1)S(1)}, bf16[160,1536]{1,0:T(8,128)(2,1)}, u32[]{:S(2)}, u32[]{:S(2)}) %collective-permute-start.20) | collective-permute-done | bytes 491552 | tf_op jit(solution)/shard_map/ppermute | solution.py:326
  28.5 1.3 collective-permute-start.11
  29.8 1.7 collective-permute-start.23
  32.5 7.2 %collective-permute-done.11.refs_11_ = bf16[128,1280]{1,0:T(8,128)(2,1)} collective-permute-done((bf16[128,1280]{1,0:T(8,128)(2,1)}, bf16[128,1280]{1,0:T(8,128)(2,1)}, u32[]{:S(2)}, u32[]{:S(2)}) %collective-permute-start.11) | collective-permute-done | bytes 327712 | tf_op jit(solution)/shard_map/ppermute | solution.py:365
  40.2 3.5 %collective-permute-done.22.refs_0_.refs_6_ = bf16[160,1536]{1,0:T(8,128)(2,1)S(1)} collective-permute-done((bf16[160,1536]{1,0:T(8,128)(2,1)}, bf16[160,1536]{1,0:T(8,128)(2,1)S(1)}, u32[]{:S(2)}, u32[]{:S(2)}) %collective-permute-start.22) | collective-permute-done | bytes 491552 | tf_op jit(solution)/shard_map/ppermute | solution.py:326
  44.2 1.2 collective-permute-start.2
  46.5 1.0 copy-done.1
  47.5 1.0 copy-done.3
  49.2 5.5 %project.3 = (bf16[128,1536]{1,0:T(8,128)(2,1)S(1)}, bf16[128,1536]{1,0:T(8,128)(2,1)}, bf16[128,1536]{1,0:T(8,128)(2,1)}, bf16[128,1536]{1,0:T(8,128)(2,1)S(1)}) custom-call(s32[3]{0:T(128)S(1)} %pad_add_fusion.index, bf16[160,1536]{1,0:T(8,128)(2,1)S(1)} %get-tuple-element.85.refs_0_, bf16[160,1536]{1,0:T(8,128)(2,1)S(1)} %get-tuple-element.86.refs_1_, ...), custom_call_target="tpu_custom_call" | custom-call | flops 2013265920 | bytes 3932160 | tf_op jit(solution)/shard_map/project/pallas_call | solution.py:290
  54.7 2.9 %collective-permute-start.24 = (bf16[128,1536]{1,0:T(8,128)(2,1)}, bf16[128,1536]{1,0:T(8,128)(2,1)S(1)}, u32[]{:S(2)}, u32[]{:S(2)}) collective-permute-start(bf16[128,1536]{1,0:T(8,128)(2,1)} %get-tuple-element.54), channel_id=1, source_target_pairs={{0,8},{2,10},{4,12},{6,14},{8,0},{10,2},{12,4},{14,6},{16,24},{18,... | collective-permute-start | bytes 1179656 | tf_op jit(solution)/shard_map/ppermute | solution.py:380
  58.5 0.9 add.95
  60.7 1.5 collective-permute-start.6
  62.3 4.4 %collective-permute-done.24 = bf16[128,1536]{1,0:T(8,128)(2,1)S(1)} collective-permute-done((bf16[128,1536]{1,0:T(8,128)(2,1)}, bf16[128,1536]{1,0:T(8,128)(2,1)S(1)}, u32[]{:S(2)}, u32[]{:S(2)}) %collective-permute-start.24) | collective-permute-done | bytes 393248 | tf_op jit(solution)/shard_map/ppermute | solution.py:380
  66.7 1.1 collective-permute-start.7
  68.0 2.2 %collective-permute-start.27 = (bf16[128,1536]{1,0:T(8,128)(2,1)S(1)}, bf16[128,1536]{1,0:T(8,128)(2,1)S(1)}, u32[]{:S(2)}, u32[]{:S(2)}) collective-permute-start(bf16[128,1536]{1,0:T(8,128)(2,1)S(1)} %add_convert_fusion), channel_id=1, source_target_pairs={{0,16},{2,18},{4,20},{6,22},{16,0},{18,2},{20,4},{22,6},{8,24},{10... | collective-permute-start | bytes 1179656 | tf_op jit(solution)/shard_map/ppermute | solution.py:380
  70.2 3.5 %collective-permute-done.3.refs_3_ = bf16[160,1536]{1,0:T(8,128)(2,1)} collective-permute-done((bf16[160,1536]{1,0:T(8,128)(2,1)S(1)}, bf16[160,1536]{1,0:T(8,128)(2,1)}, u32[]{:S(2)}, u32[]{:S(2)}) %collective-permute-start.3) | collective-permute-done | bytes 491552 | tf_op jit(solution)/shard_map/ppermute | solution.py:326
  73.7 3.7 %collective-permute-start.26 = (bf16[128,1536]{1,0:T(8,128)(2,1)}, bf16[128,1536]{1,0:T(8,128)(2,1)S(1)}, u32[]{:S(2)}, u32[]{:S(2)}) collective-permute-start(bf16[128,1536]{1,0:T(8,128)(2,1)} %get-tuple-element.57), channel_id=1, source_target_pairs={{0,8},{2,10},{4,12},{6,14},{24,16},{26,18},{28,20},{30,22},{1,9},{... | collective-permute-start | bytes 1179656 | tf_op jit(solution)/shard_map/ppermute | solution.py:380
  77.5 5.8 %collective-permute-done.6.refs_6_ = bf16[160,1536]{1,0:T(8,128)(2,1)} collective-permute-done((bf16[160,1536]{1,0:T(8,128)(2,1)}, bf16[160,1536]{1,0:T(8,128)(2,1)}, u32[]{:S(2)}, u32[]{:S(2)}) %collective-permute-start.6) | collective-permute-done | bytes 491552 | tf_op jit(solution)/shard_map/ppermute | solution.py:326
  83.2 5.9 %project.2 = (bf16[128,1536]{1,0:T(8,128)(2,1)S(1)}, bf16[128,1536]{1,0:T(8,128)(2,1)}, bf16[128,1536]{1,0:T(8,128)(2,1)}, bf16[128,1536]{1,0:T(8,128)(2,1)S(1)}) custom-call(s32[3]{0:T(128)S(1)} %pad_add_fusion.index, bf16[160,1536]{1,0:T(8,128)(2,1)S(1)} %get-tuple-element.44.refs_0_, bf16[160,1536]{1,0:T(8,128)(2,1)S(1)} %get-tuple-element.45.refs_1_, ...), custom_call_target="tpu_custom_call" | custom-call | flops 2013265920 | bytes 3932160 | tf_op jit(solution)/shard_map/project/pallas_call | solution.py:290
  89.1 1.5 collective-permute-start.16
  91.4 1.4 pack.2
  92.8 5.0 %all-to-all-start = ((bf16[16,16,1152]{2,1,0:T(8,128)(2,1)}), bf16[16,16,1152]{2,1,0:T(8,128)(2,1)S(1)}, u32[]{:S(2)}, u32[]{:S(2)}) async-start(bf16[16,16,1152]{2,1,0:T(8,128)(2,1)} %bitcast.7), calls=%async_computation | async-start | bytes 1179648 | tf_op jit(solution)/shard_map/all_to_all | solution.py:417
  97.8 1.3 collective-permute-done.16
  99.1 1.9 %add_convert_fusion.1 = bf16[128,1536]{1,0:T(8,128)(2,1)} fusion(bf16[128,1536]{1,0:T(8,128)(2,1)} %collective-permute-done.16, bf16[128,1536]{1,0:T(8,128)(2,1)S(1)} %get-tuple-element.52, pred[]{:T(512)S(6)} %or.2), kind=kLoop, calls=%fused_computation.2 | loop fusion | flops 983040 | bytes 1179649 | tf_op jit(solution)/shard_map/convert_element_type | solution.py:387
  101.0 17.4 %collective-permute-start.19 = (bf16[128,1536]{1,0:T(8,128)(2,1)}, bf16[128,1536]{1,0:T(8,128)(2,1)S(1)}, u32[]{:S(2)}, u32[]{:S(2)}) collective-permute-start(bf16[128,1536]{1,0:T(8,128)(2,1)} %add_convert_fusion.1), channel_id=1, source_target_pairs={{0,16},{2,18},{4,20},{6,22},{16,0},{18,2},{20,4},{22,6},{8,24},{10... | collective-permute-start | bytes 1179656 | tf_op jit(solution)/shard_map/ppermute | solution.py:380
  118.4 1.5 collective-permute-start.18
  119.8 1.0 broadcast_select_fusion.2.refs_1_
  120.9 1.6 copy-done.7
  122.5 1.6 copy-done.9
  124.1 8.0 %prefix_part.2 = bf16[256,1152]{1,0:T(8,128)(2,1)} custom-call(bf16[256,1152]{1,0:T(8,128)(2,1)S(1)} %bitcast.25, bf16[256,1152]{1,0:T(8,128)(2,1)S(1)} %bitcast.26, bf16[2048,512]{1,0:T(8,128)(2,1)S(1)} %bitcast.30, bf16[2048,512]{1,0:T(8,128)(2,1)S(1)} %bitcast.32), custom_call_target="tpu_custom_call" | custom-call | flops 2147483648 | bytes 2097152 | tf_op jit(solution)/shard_map/prefix_part/pallas_call | solution.py:83
  132.6 16.6 %all_to_all.20 = bf16[16,16,1024]{2,1,0:T(8,128)(2,1)S(1)} all-to-all(bf16[16,16,1024]{2,1,0:T(8,128)(2,1)S(1)} %bitcast.28), channel_id=1, replica_groups=mesh['wide'=16,'narrow'=2] {'wide'}, dimensions={0} | all-to-all | bytes 1048576 | tf_op jit(solution)/shard_map/all_to_all | solution.py:417
  149.2 4.0 %all-to-all-start.1 = ((bf16[16,16,1152]{2,1,0:T(8,128)(2,1)}), bf16[16,16,1152]{2,1,0:T(8,128)(2,1)S(1)}, u32[]{:S(2)}, u32[]{:S(2)}) async-start(bf16[16,16,1152]{2,1,0:T(8,128)(2,1)} %bitcast.11), calls=%async_computation.1 | async-start | bytes 1179648 | tf_op jit(solution)/shard_map/all_to_all | solution.py:417
  153.3 1.6 copy-done.8
  154.9 1.6 copy-done.10
  156.4 7.9 %prefix_part.3 = bf16[256,1152]{1,0:T(8,128)(2,1)} custom-call(bf16[256,1024]{1,0:T(8,128)(2,1)S(1)} %bitcast.29, bf16[256,1152]{1,0:T(8,128)(2,1)S(1)} %bitcast.27, bf16[2048,512]{1,0:T(8,128)(2,1)S(1)} %bitcast.31, bf16[2048,512]{1,0:T(8,128)(2,1)S(1)} %bitcast.33), custom_call_target="tpu_custom_call" | custom-call | flops 2147483648 | bytes 2097152 | tf_op jit(solution)/shard_map/prefix_part/pallas_call | solution.py:83
  164.7 6.6 %all-to-all-start.3 = ((bf16[16,16,1152]{2,1,0:T(8,128)(2,1)}), bf16[16,16,1152]{2,1,0:T(8,128)(2,1)S(1)}, u32[]{:S(2)}, u32[]{:S(2)}) async-start(bf16[16,16,1152]{2,1,0:T(8,128)(2,1)} %bitcast.15), calls=%async_computation.3 | async-start | bytes 1179648 | tf_op jit(solution)/shard_map/all_to_all | solution.py:417
  171.3 2.0 %near_part.2 = (f32[128,1024]{1,0:T(8,128)S(1)}, f32[128,128]{1,0:T(8,128)S(1)}) custom-call(bf16[128,1024]{1,0:T(8,128)(2,1)S(1)} %get-tuple-element.67.query, bf16[128,256]{1,0:T(8,128)(2,1)S(1)} %get-tuple-element.68.key, bf16[128,256]{1,0:T(8,128)(2,1)S(1)} %get-tuple-element.69.value), custom_call_target="tpu_custom_call" | custom-call | flops 67108864 | bytes 1048576 | tf_op jit(solution)/shard_map/near_part/pallas_call | solution.py:180
  173.4 2.0 %near_part.3 = (f32[128,1024]{1,0:T(8,128)S(1)}, f32[128,128]{1,0:T(8,128)S(1)}) custom-call(bf16[128,1024]{1,0:T(8,128)(2,1)S(1)} %copy-done.5, bf16[128,256]{1,0:T(8,128)(2,1)S(1)} %get-tuple-element.79.key, bf16[128,256]{1,0:T(8,128)(2,1)S(1)} %get-tuple-element.80.value), custom_call_target="tpu_custom_call" | custom-call | flops 67108864 | bytes 1048576 | tf_op jit(solution)/shard_map/near_part/pallas_call | solution.py:180
  175.4 1.5 join.2
  176.8 5.9 %all-to-all-done.3 = bf16[16,16,1152]{2,1,0:T(8,128)(2,1)S(1)} async-done(((bf16[16,16,1152]{2,1,0:T(8,128)(2,1)}), bf16[16,16,1152]{2,1,0:T(8,128)(2,1)S(1)}, u32[]{:S(2)}, u32[]{:S(2)}) %all-to-all-start.3) | async-done | bytes 589856 | tf_op jit(solution)/shard_map/all_to_all | solution.py:417
  182.7 1.5 join.3
  184.3 1.1 reshape.150
  (90 shorter events, 13.0 us)
Async XLA Ops:
  0.0 7.4 %copy-start.14 = (s32[64,1]{0,1:T(1,128)S(1)}, s32[64,1]{0,1:T(1,128)}, u32[]{:S(2)}) copy-start(s32[64,1]{0,1:T(1,128)} %param.10) | copy-start | bytes 772
  0.0 9.9 %copy-start.13 = (bf16[64,2,2560]{2,1,0:T(2,128)(2,1)S(1)}, bf16[64,2,2560]{2,1,0:T(2,128)(2,1)}, u32[]{:S(2)}) copy-start(bf16[64,2,2560]{2,1,0:T(2,128)(2,1)} %param.6) | copy-start | bytes 1966084
  1.7 13.2 %copy-start.15 = (s32[64]{0:T(128)S(1)}, s32[64]{0:T(128)}, u32[]{:S(2)}) copy-start(s32[64]{0:T(128)} %param.11) | copy-start | bytes 772
  1.7 28.1 %collective-permute-start.21 = (bf16[160,1536]{1,0:T(8,128)(2,1)S(1)}, bf16[160,1536]{1,0:T(8,128)(2,1)}, u32[]{:S(2)}, u32[]{:S(2)}) collective-permute-start(bf16[160,1536]{1,0:T(8,128)(2,1)S(1)} %get-tuple-element.86.refs_1_), channel_id=1, source_target_pairs={{0,4},{2,6},{4,0},{6,2},{8,12},{10,14},{12,8},{14,10},{16,20},{18,... | collective-permute-start | bytes 1474568 | tf_op jit(solution)/shard_map/ppermute | solution.py:326
  4.7 34.9 %collective-permute-start = (bf16[160,1536]{1,0:T(8,128)(2,1)S(1)}, bf16[160,1536]{1,0:T(8,128)(2,1)}, u32[]{:S(2)}, u32[]{:S(2)}) collective-permute-start(bf16[160,1536]{1,0:T(8,128)(2,1)S(1)} %get-tuple-element.86.refs_1_), channel_id=1, source_target_pairs={{0,2},{2,0},{4,6},{6,4},{8,10},{10,8},{12,14},{14,12},{16,18},{18,... | collective-permute-start | bytes 1474568 | tf_op jit(solution)/shard_map/ppermute | solution.py:326
  6.9 1.2 collective-permute-start.8
  6.9 21.1 %collective-permute-start.20 = (bf16[160,1536]{1,0:T(8,128)(2,1)S(1)}, bf16[160,1536]{1,0:T(8,128)(2,1)}, u32[]{:S(2)}, u32[]{:S(2)}) collective-permute-start(bf16[160,1536]{1,0:T(8,128)(2,1)S(1)} %get-tuple-element.85.refs_0_), channel_id=1, source_target_pairs={{0,2},{2,0},{4,6},{6,4},{8,10},{10,8},{12,14},{14,12},{16,18},{18,... | collective-permute-start | bytes 1474568 | tf_op jit(solution)/shard_map/ppermute | solution.py:326
  11.4 9.3 %collective-permute-start.9 = (bf16[128,1280]{1,0:T(8,128)(2,1)}, bf16[128,1280]{1,0:T(8,128)(2,1)}, u32[]{:S(2)}, u32[]{:S(2)}) collective-permute-start(bf16[128,1280]{1,0:T(8,128)(2,1)} %get-tuple-element.89), channel_id=1, source_target_pairs={{0,8},{2,10},{4,12},{6,14},{8,0},{10,2},{12,4},{14,6},{17,25},{19,... | collective-permute-start | bytes 983048 | tf_op jit(solution)/shard_map/ppermute | solution.py:365
  15.0 13.5 %collective-permute-start.10 = (bf16[128,1280]{1,0:T(8,128)(2,1)S(1)}, bf16[128,1280]{1,0:T(8,128)(2,1)}, u32[]{:S(2)}, u32[]{:S(2)}) collective-permute-start(bf16[128,1280]{1,0:T(8,128)(2,1)S(1)} %get-tuple-element.90.refs_8_), channel_id=1, source_target_pairs={{1,17},{3,19},{5,21},{7,23},{9,25},{11,27},{13,29},{15,31},{16,0},... | collective-permute-start | bytes 983048 | tf_op jit(solution)/shard_map/ppermute | solution.py:365
  20.7 19.4 %collective-permute-start.1 = (bf16[160,1536]{1,0:T(8,128)(2,1)S(1)}, bf16[160,1536]{1,0:T(8,128)(2,1)}, u32[]{:S(2)}, u32[]{:S(2)}) collective-permute-start(bf16[160,1536]{1,0:T(8,128)(2,1)S(1)} %get-tuple-element.85.refs_0_), channel_id=1, source_target_pairs={{0,4},{2,6},{4,0},{6,2},{8,12},{10,14},{12,8},{14,10},{16,20},{18,... | collective-permute-start | bytes 1474568 | tf_op jit(solution)/shard_map/ppermute | solution.py:326
  28.0 15.7 %collective-permute-start.22 = (bf16[160,1536]{1,0:T(8,128)(2,1)}, bf16[160,1536]{1,0:T(8,128)(2,1)S(1)}, u32[]{:S(2)}, u32[]{:S(2)}) collective-permute-start(bf16[160,1536]{1,0:T(8,128)(2,1)} %collective-permute-done.20.refs_2_), channel_id=1, source_target_pairs={{0,4},{2,6},{4,0},{6,2},{8,12},{10,14},{12,8},{14,10},{16,20},{18,... | collective-permute-start | bytes 1474568 | tf_op jit(solution)/shard_map/ppermute | solution.py:326
  28.5 11.2 %collective-permute-start.11 = (bf16[128,1280]{1,0:T(8,128)(2,1)}, bf16[128,1280]{1,0:T(8,128)(2,1)}, u32[]{:S(2)}, u32[]{:S(2)}) collective-permute-start(bf16[128,1280]{1,0:T(8,128)(2,1)} %get-tuple-element.89), channel_id=1, source_target_pairs={{1,25},{3,27},{5,29},{7,31},{9,17},{11,19},{13,21},{15,23},{16,8},... | collective-permute-start | bytes 983048 | tf_op jit(solution)/shard_map/ppermute | solution.py:365
  29.8 14.4 %collective-permute-start.23 = (bf16[160,1536]{1,0:T(8,128)(2,1)}, bf16[160,1536]{1,0:T(8,128)(2,1)S(1)}, u32[]{:S(2)}, u32[]{:S(2)}) collective-permute-start(bf16[160,1536]{1,0:T(8,128)(2,1)} %collective-permute-done.21.refs_5_), channel_id=1, source_target_pairs={{0,2},{2,0},{4,6},{6,4},{8,10},{10,8},{12,14},{14,12},{16,18},{18,... | collective-permute-start | bytes 1474568 | tf_op jit(solution)/shard_map/ppermute | solution.py:326
  39.6 6.3 %collective-permute-start.12 = (bf16[128,1280]{1,0:T(8,128)(2,1)S(1)}, bf16[128,1280]{1,0:T(8,128)(2,1)}, u32[]{:S(2)}, u32[]{:S(2)}) collective-permute-start(bf16[128,1280]{1,0:T(8,128)(2,1)S(1)} %get-tuple-element.90.refs_8_), channel_id=1, source_target_pairs={{0,1},{1,0},{2,3},{3,2},{4,5},{5,4},{6,7},{7,6},{8,9},{9,8},{10,11... | collective-permute-start | bytes 983048 | tf_op jit(solution)/shard_map/ppermute | solution.py:370
  39.6 6.8 %collective-permute-start.13 = (bf16[128,1280]{1,0:T(8,128)(2,1)}, bf16[128,1280]{1,0:T(8,128)(2,1)}, u32[]{:S(2)}, u32[]{:S(2)}) collective-permute-start(bf16[128,1280]{1,0:T(8,128)(2,1)} %collective-permute-done.9.refs_9_), channel_id=1, source_target_pairs={{0,1},{1,0},{2,3},{3,2},{4,5},{5,4},{6,7},{7,6},{8,9},{9,8},{10,11... | collective-permute-start | bytes 983048 | tf_op jit(solution)/shard_map/ppermute | solution.py:370
  40.2 6.3 %collective-permute-start.14 = (bf16[128,1280]{1,0:T(8,128)(2,1)}, bf16[128,1280]{1,0:T(8,128)(2,1)}, u32[]{:S(2)}, u32[]{:S(2)}) collective-permute-start(bf16[128,1280]{1,0:T(8,128)(2,1)} %collective-permute-done.10.refs_10_), channel_id=1, source_target_pairs={{0,1},{1,0},{2,3},{3,2},{4,5},{5,4},{6,7},{7,6},{8,9},{9,8},{10,11... | collective-permute-start | bytes 983048 | tf_op jit(solution)/shard_map/ppermute | solution.py:370
  43.8 1.6 copy-start
  43.8 2.7 %collective-permute-start.15 = (bf16[128,1280]{1,0:T(8,128)(2,1)}, bf16[128,1280]{1,0:T(8,128)(2,1)}, u32[]{:S(2)}, u32[]{:S(2)}) collective-permute-start(bf16[128,1280]{1,0:T(8,128)(2,1)} %collective-permute-done.11.refs_11_), channel_id=1, source_target_pairs={{0,1},{1,0},{2,3},{3,2},{4,5},{5,4},{6,7},{7,6},{8,9},{9,8},{10,11... | collective-permute-start | bytes 983048 | tf_op jit(solution)/shard_map/ppermute | solution.py:370
  44.2 1.2 copy-start.2
  44.2 16.1 %collective-permute-start.2 = (bf16[160,1536]{1,0:T(8,128)(2,1)S(1)}, bf16[160,1536]{1,0:T(8,128)(2,1)}, u32[]{:S(2)}, u32[]{:S(2)}) collective-permute-start(bf16[160,1536]{1,0:T(8,128)(2,1)S(1)} %get-tuple-element.44.refs_0_), channel_id=1, source_target_pairs={{0,2},{2,0},{4,6},{6,4},{8,10},{10,8},{12,14},{14,12},{16,18},{18,... | collective-permute-start | bytes 1474568 | tf_op jit(solution)/shard_map/ppermute | solution.py:326
  45.9 14.8 %collective-permute-start.5 = (bf16[160,1536]{1,0:T(8,128)(2,1)S(1)}, bf16[160,1536]{1,0:T(8,128)(2,1)}, u32[]{:S(2)}, u32[]{:S(2)}) collective-permute-start(bf16[160,1536]{1,0:T(8,128)(2,1)S(1)} %get-tuple-element.45.refs_1_), channel_id=1, source_target_pairs={{0,4},{2,6},{4,0},{6,2},{8,12},{10,14},{12,8},{14,10},{16,20},{18,... | collective-permute-start | bytes 1474568 | tf_op jit(solution)/shard_map/ppermute | solution.py:326
  46.5 1.0 copy-start.1
  47.5 1.0 copy-start.3
  48.5 0.7 copy-start.6
  54.7 11.9 %collective-permute-start.24 = (bf16[128,1536]{1,0:T(8,128)(2,1)}, bf16[128,1536]{1,0:T(8,128)(2,1)S(1)}, u32[]{:S(2)}, u32[]{:S(2)}) collective-permute-start(bf16[128,1536]{1,0:T(8,128)(2,1)} %get-tuple-element.54), channel_id=1, source_target_pairs={{0,8},{2,10},{4,12},{6,14},{8,0},{10,2},{12,4},{14,6},{16,24},{18,... | collective-permute-start | bytes 1179656 | tf_op jit(solution)/shard_map/ppermute | solution.py:380
  57.7 10.2 %collective-permute-start.25 = (bf16[128,1536]{1,0:T(8,128)(2,1)}, bf16[128,1536]{1,0:T(8,128)(2,1)S(1)}, u32[]{:S(2)}, u32[]{:S(2)}) collective-permute-start(bf16[128,1536]{1,0:T(8,128)(2,1)} %get-tuple-element.57), channel_id=1, source_target_pairs={{8,16},{10,18},{12,20},{14,22},{16,8},{18,10},{20,12},{22,14},{9,1... | collective-permute-start | bytes 1179656 | tf_op jit(solution)/shard_map/ppermute | solution.py:380
  59.4 14.3 %collective-permute-start.3 = (bf16[160,1536]{1,0:T(8,128)(2,1)S(1)}, bf16[160,1536]{1,0:T(8,128)(2,1)}, u32[]{:S(2)}, u32[]{:S(2)}) collective-permute-start(bf16[160,1536]{1,0:T(8,128)(2,1)S(1)} %get-tuple-element.45.refs_1_), channel_id=1, source_target_pairs={{0,2},{2,0},{4,6},{6,4},{8,10},{10,8},{12,14},{14,12},{16,18},{18,... | collective-permute-start | bytes 1474568 | tf_op jit(solution)/shard_map/ppermute | solution.py:326
  60.2 17.2 %collective-permute-start.4 = (bf16[160,1536]{1,0:T(8,128)(2,1)S(1)}, bf16[160,1536]{1,0:T(8,128)(2,1)}, u32[]{:S(2)}, u32[]{:S(2)}) collective-permute-start(bf16[160,1536]{1,0:T(8,128)(2,1)S(1)} %get-tuple-element.44.refs_0_), channel_id=1, source_target_pairs={{0,4},{2,6},{4,0},{6,2},{8,12},{10,14},{12,8},{14,10},{16,20},{18,... | collective-permute-start | bytes 1474568 | tf_op jit(solution)/shard_map/ppermute | solution.py:326
  60.7 22.5 %collective-permute-start.6 = (bf16[160,1536]{1,0:T(8,128)(2,1)}, bf16[160,1536]{1,0:T(8,128)(2,1)}, u32[]{:S(2)}, u32[]{:S(2)}) collective-permute-start(bf16[160,1536]{1,0:T(8,128)(2,1)} %collective-permute-done.2.refs_2_), channel_id=1, source_target_pairs={{0,4},{2,6},{4,0},{6,2},{8,12},{10,14},{12,8},{14,10},{16,20},{18,... | collective-permute-start | bytes 1474568 | tf_op jit(solution)/shard_map/ppermute | solution.py:326
  66.7 16.6 %copy-start.11 = (bf16[128,1536]{1,0:T(8,128)(2,1)}, bf16[128,1536]{1,0:T(8,128)(2,1)S(1)}, u32[]{:S(2)}) copy-start(bf16[128,1536]{1,0:T(8,128)(2,1)S(1)} %collective-permute-done.24) | copy-start | bytes 1179652
  66.7 16.6 %collective-permute-start.7 = (bf16[160,1536]{1,0:T(8,128)(2,1)}, bf16[160,1536]{1,0:T(8,128)(2,1)}, u32[]{:S(2)}, u32[]{:S(2)}) collective-permute-start(bf16[160,1536]{1,0:T(8,128)(2,1)} %collective-permute-done.5.refs_5_), channel_id=1, source_target_pairs={{0,2},{2,0},{4,6},{6,4},{8,10},{10,8},{12,14},{14,12},{16,18},{18,... | collective-permute-start | bytes 1474568 | tf_op jit(solution)/shard_map/ppermute | solution.py:326
  68.0 23.4 %collective-permute-start.27 = (bf16[128,1536]{1,0:T(8,128)(2,1)S(1)}, bf16[128,1536]{1,0:T(8,128)(2,1)S(1)}, u32[]{:S(2)}, u32[]{:S(2)}) collective-permute-start(bf16[128,1536]{1,0:T(8,128)(2,1)S(1)} %add_convert_fusion), channel_id=1, source_target_pairs={{0,16},{2,18},{4,20},{6,22},{16,0},{18,2},{20,4},{22,6},{8,24},{10... | collective-permute-start | bytes 1179656 | tf_op jit(solution)/shard_map/ppermute | solution.py:380
  73.7 17.7 %collective-permute-start.26 = (bf16[128,1536]{1,0:T(8,128)(2,1)}, bf16[128,1536]{1,0:T(8,128)(2,1)S(1)}, u32[]{:S(2)}, u32[]{:S(2)}) collective-permute-start(bf16[128,1536]{1,0:T(8,128)(2,1)} %get-tuple-element.57), channel_id=1, source_target_pairs={{0,8},{2,10},{4,12},{6,14},{24,16},{26,18},{28,20},{30,22},{1,9},{... | collective-permute-start | bytes 1179656 | tf_op jit(solution)/shard_map/ppermute | solution.py:380
  83.2 8.1 %copy-start.12 = (bf16[128,1536]{1,0:T(8,128)(2,1)S(1)}, bf16[128,1536]{1,0:T(8,128)(2,1)}, u32[]{:S(2)}) copy-start(bf16[128,1536]{1,0:T(8,128)(2,1)} %copy-done.11) | copy-start | bytes 1179652
  89.1 10.0 %collective-permute-start.16 = (bf16[128,1536]{1,0:T(8,128)(2,1)}, bf16[128,1536]{1,0:T(8,128)(2,1)}, u32[]{:S(2)}, u32[]{:S(2)}) collective-permute-start(bf16[128,1536]{1,0:T(8,128)(2,1)} %get-tuple-element.47), channel_id=1, source_target_pairs={{0,8},{2,10},{4,12},{6,14},{8,0},{10,2},{12,4},{14,6},{16,24},{18,... | collective-permute-start | bytes 1179656 | tf_op jit(solution)/shard_map/ppermute | solution.py:380
  90.6 8.5 %collective-permute-start.17 = (bf16[128,1536]{1,0:T(8,128)(2,1)}, bf16[128,1536]{1,0:T(8,128)(2,1)S(1)}, u32[]{:S(2)}, u32[]{:S(2)}) collective-permute-start(bf16[128,1536]{1,0:T(8,128)(2,1)} %get-tuple-element.50), channel_id=1, source_target_pairs={{8,16},{10,18},{12,20},{14,22},{16,8},{18,10},{20,12},{22,14},{9,1... | collective-permute-start | bytes 1179656 | tf_op jit(solution)/shard_map/ppermute | solution.py:380
  92.8 28.1 %all-to-all-start = ((bf16[16,16,1152]{2,1,0:T(8,128)(2,1)}), bf16[16,16,1152]{2,1,0:T(8,128)(2,1)S(1)}, u32[]{:S(2)}, u32[]{:S(2)}) async-start(bf16[16,16,1152]{2,1,0:T(8,128)(2,1)} %bitcast.7), calls=%async_computation | async-start | bytes 1179648 | tf_op jit(solution)/shard_map/all_to_all | solution.py:417
  101.0 31.1 %collective-permute-start.19 = (bf16[128,1536]{1,0:T(8,128)(2,1)}, bf16[128,1536]{1,0:T(8,128)(2,1)S(1)}, u32[]{:S(2)}, u32[]{:S(2)}) collective-permute-start(bf16[128,1536]{1,0:T(8,128)(2,1)} %add_convert_fusion.1), channel_id=1, source_target_pairs={{0,16},{2,18},{4,20},{6,22},{16,0},{18,2},{20,4},{22,6},{8,24},{10... | collective-permute-start | bytes 1179656 | tf_op jit(solution)/shard_map/ppermute | solution.py:380
  118.4 13.7 %collective-permute-start.18 = (bf16[128,1536]{1,0:T(8,128)(2,1)}, bf16[128,1536]{1,0:T(8,128)(2,1)S(1)}, u32[]{:S(2)}, u32[]{:S(2)}) collective-permute-start(bf16[128,1536]{1,0:T(8,128)(2,1)} %get-tuple-element.50), channel_id=1, source_target_pairs={{0,8},{2,10},{4,12},{6,14},{24,16},{26,18},{28,20},{30,22},{1,9},{... | collective-permute-start | bytes 1179656 | tf_op jit(solution)/shard_map/ppermute | solution.py:380
  120.9 1.6 copy-start.7
  122.5 1.6 copy-start.9
  132.6 16.6 %copy-start.4 = (bf16[128,1024]{1,0:T(8,128)(2,1)}, bf16[128,1024]{1,0:T(8,128)(2,1)S(1)}, u32[]{:S(2)}) copy-start(bf16[128,1024]{1,0:T(8,128)(2,1)S(1)} %get-tuple-element.78.query) | copy-start | bytes 786436
  149.2 15.5 %all-to-all-start.1 = ((bf16[16,16,1152]{2,1,0:T(8,128)(2,1)}), bf16[16,16,1152]{2,1,0:T(8,128)(2,1)S(1)}, u32[]{:S(2)}, u32[]{:S(2)}) async-start(bf16[16,16,1152]{2,1,0:T(8,128)(2,1)} %bitcast.11), calls=%async_computation.1 | async-start | bytes 1179648 | tf_op jit(solution)/shard_map/all_to_all | solution.py:417
  153.3 1.6 copy-start.8
  154.8 1.6 copy-start.10
  156.4 16.9 %copy-start.5 = (bf16[128,1024]{1,0:T(8,128)(2,1)S(1)}, bf16[128,1024]{1,0:T(8,128)(2,1)}, u32[]{:S(2)}) copy-start(bf16[128,1024]{1,0:T(8,128)(2,1)} %copy-done.4) | copy-start | bytes 786436
  164.7 18.1 %all-to-all-start.3 = ((bf16[16,16,1152]{2,1,0:T(8,128)(2,1)}), bf16[16,16,1152]{2,1,0:T(8,128)(2,1)S(1)}, u32[]{:S(2)}, u32[]{:S(2)}) async-start(bf16[16,16,1152]{2,1,0:T(8,128)(2,1)} %bitcast.15), calls=%async_computation.3 | async-start | bytes 1179648 | tf_op jit(solution)/shard_map/all_to_all | solution.py:417
